TPU v7x, 256 devices: a whole 4x4x8 slice. The times are simulated.
256 devices in a mesh: dp: 32 (over z, x_hi, core), mp: 8 (over y, x_lo).
Axes of the slice: x: 4 (x_hi: 2, x_lo: 2; x = x_hi * 2 + x_lo), y: 4, z: 8, core: 2. Of those that a mesh axis runs over, the one named last changes fastest.
Arguments:
- train_x: bfloat16 [256, 8192], P('mp', 'dp'), may hold values from -6 to 6
- train_cot: bfloat16 [256, 8192], P('mp', 'dp'), may hold values from -6 to 6
- val_x: bfloat16 [32, 8192], P('mp', 'dp'), may hold values from -6 to 6
- val_cot: bfloat16 [32, 8192], P('mp', 'dp'), may hold values from -6 to 6
- w_gate: bfloat16 [8192, 14336], P('dp', 'mp'), may hold values from -0.0625 to 0.0625
- w_up: bfloat16 [8192, 14336], P('dp', 'mp'), may hold values from -0.0625 to 0.0625
- w_down: bfloat16 [14336, 8192], P('mp', 'dp'), may hold values from -0.046875 to 0.046875
- step_weights: float32 [8], replicated, may hold values from 0.25 to 4
- example_ids: int32 [256], replicated, may hold values from 0 to 7, never falling along the last dimension, each value on 1 to 64 neighbouring positions
- val_mask: int32 [32], replicated, may hold values 0 or 1
Outputs:
- grad_gate: bfloat16 [8192, 14336], P('dp', 'mp')
- grad_up: bfloat16 [8192, 14336], P('dp', 'mp')
- grad_down: bfloat16 [14336, 8192], P('mp', 'dp')
- example_weights: float32 [8], replicated
Inputs may be any that keep to these rules, and one draw needn't show every extreme that they name: `example_ids`: never falling along the tokens; each example holds 1 to 64 tokens, one exactly 64.
All inputs are finite; a program needn't handle non-finite values.
Results may differ from a plain program's by a relative error of at most 0.006.
Values may be sent and summed in bfloat16 or wider, within the bound.
A program may use at most 64 MiB of HBM per device.

v0:
```python
import functools

import jax
import jax.numpy as jnp
from jax import lax
from jax.sharding import Mesh
from jax.sharding import PartitionSpec as P

DP = ("dp_0", "dp_1", "dp_2")
MP = ("mp_0", "mp_1")
DP_MP = ("dp_0", "dp_1", "dp_2", "mp_0", "mp_1")


LEARN_RATE = 0.0003


def split_up(array, dim, size):
    dims = array.shape
    blocks = array.reshape(*dims[:dim], size, dims[dim] // size, *dims[dim + 1 :])
    return jnp.moveaxis(blocks, dim, 0)


def sent_and_summed(array, axis, dim):
    size = lax.axis_size(axis)
    blocks = lax.all_to_all(split_up(array, dim, size), axis, 0, 0, tiled=True)
    return jnp.sum(blocks, axis=0)


def sum_in_two_steps(array, axes, dim):
    far, near = axes
    own = sent_and_summed(split_up(array, dim, lax.axis_size(far)), near, dim + 1)
    return jnp.sum(lax.all_to_all(own, far, 0, 0, tiled=True), axis=0)


def from_everyone(array, axis):
    copies = jnp.broadcast_to(array, (lax.axis_size(axis), *array.shape))
    return lax.all_to_all(copies, axis, split_axis=0, concat_axis=0, tiled=True)


def in_order(blocks, dim):
    dims = list(blocks.shape[1:])
    dims[dim] *= blocks.shape[0]
    return jnp.moveaxis(blocks, 0, dim).reshape(dims)


def whole_of(array, axes, dim):
    far, near = axes
    first = from_everyone(array, far)
    blocks = jnp.swapaxes(from_everyone(first, near), 0, 1)
    return in_order(blocks.reshape(-1, *array.shape), dim)


def side_by_side(arrays, axis, dim, along):
    widths = [a.shape[along] for a in arrays]
    both = jnp.concatenate(arrays, axis=along)
    out = lax.all_gather(both, axis, axis=dim, tiled=True)
    return tuple(jnp.split(out, [sum(widths[:k]) for k in range(1, len(widths))], axis=along))


def over_axes(array, axes):
    return functools.reduce(lax.psum, axes, array)


def contract_rows(left, right):
    return lax.dot_general(
        left, right, (((0,), (0,)), ((), ())), preferred_element_type=jnp.float32
    )


def contract_width(left, right):
    return lax.dot_general(
        left, right, (((1,), (1,)), ((), ())), preferred_element_type=jnp.float32
    )


def three_products(inputs, cotangent, first, second, third):
    left = jnp.dot(inputs, first, preferred_element_type=jnp.float32)
    middle = jnp.dot(inputs, second, preferred_element_type=jnp.float32)
    right = contract_width(cotangent, third)
    return jnp.concatenate([left, middle, right], axis=1)


def hidden_terms(inputs, cotangent, w_gate, w_up, w_down):
    width = w_gate.shape[1]
    sums = sum_in_two_steps(
        three_products(inputs, cotangent, w_gate, w_up, w_down), (("dp_0", "dp_1"), "dp_2"), 0
    )
    gate = sums[:, :width]
    up = sums[:, width : 2 * width]
    back = sums[:, 2 * width :]
    sig = jax.nn.sigmoid(gate)
    act = gate * sig
    hidden = (act * up).astype(jnp.bfloat16)
    d_gate = (back * up * sig * (1.0 + gate * (1.0 - sig))).astype(jnp.bfloat16)
    d_up = (back * act).astype(jnp.bfloat16)
    mine = jnp.concatenate([hidden, d_gate, d_up], axis=1)
    whole = whole_of(mine, (("dp_0", "dp_1"), "dp_2"), 0)
    return (mine, whole)


def gradients(inputs, cotangent, whole, factor):
    width = whole.shape[1] // 3
    scaled_in = (inputs * factor[:, None]).astype(jnp.bfloat16)
    scaled_cot = (cotangent * factor[:, None]).astype(jnp.bfloat16)
    inner = contract_rows(scaled_in, whole[:, width:])
    grad_d = contract_rows(whole[:, :width], scaled_cot)
    return (inner[:, :width], inner[:, width:], grad_d)


def per_token(example_ids, table):
    labels = jnp.arange(table.shape[0], dtype=jnp.int32)
    match = example_ids[:, None] == labels[None, :]
    return jnp.sum(jnp.where(match, table[None, :], jnp.zeros((), table.dtype)), axis=1)


def token_inner(products, acts):
    width = acts.shape[1] // 3
    total = products[:, :width] * acts[:, width : 2 * width]
    total = total + products[:, width : 2 * width] * acts[:, 2 * width :]
    total = total + products[:, 2 * width :] * acts[:, :width]
    return jnp.sum(total, axis=1)


def body(
    train_x, train_cot, val_x, val_cot, w_gate, w_up, w_down, step_weights, example_ids, val_mask
):
    full_x, full_cot, full_vx, full_vcot = (
        *side_by_side((train_x, train_cot), MP, 0, 1),
        *side_by_side((val_x, val_cot), MP, 0, 1),
    )
    mine, whole = hidden_terms(full_x, full_cot, w_gate, w_up, w_down)
    factor = per_token(example_ids, step_weights)
    grad_g, grad_u, grad_d = gradients(full_x, full_cot, whole, factor)
    ahead_g = (w_gate.astype(jnp.float32) - LEARN_RATE * grad_g).astype(jnp.bfloat16)
    ahead_u = (w_up.astype(jnp.float32) - LEARN_RATE * grad_u).astype(jnp.bfloat16)
    ahead_d = (w_down.astype(jnp.float32) - LEARN_RATE * grad_d).astype(jnp.bfloat16)
    unused, val_whole = hidden_terms(full_vx, full_vcot, ahead_g, ahead_u, ahead_d)
    val_g, val_u, val_d = gradients(full_vx, full_vcot, val_whole, val_mask.astype(jnp.float32))
    val_g = val_g.astype(jnp.bfloat16)
    val_u = val_u.astype(jnp.bfloat16)
    val_d = val_d.astype(jnp.bfloat16)
    products = three_products(full_x, full_cot, val_g, val_u, val_d)
    token_score = token_inner(products, whole)
    labels = jnp.arange(step_weights.shape[0], dtype=jnp.int32)
    match = example_ids[:, None] == labels[None, :]
    partial_score = jnp.sum(
        jnp.where(match, token_score[:, None], jnp.zeros((), jnp.float32)), axis=0
    )
    score = over_axes(partial_score, DP_MP)
    spread_rms = jnp.sqrt(jnp.mean(score * score) + 1e-06)
    softened = jax.nn.softplus(score / (4.0 * spread_rms))
    weights = step_weights.shape[0] * softened / jnp.sum(softened)
    final = per_token(example_ids, weights)
    out_g, out_u, out_d = gradients(full_x, full_cot, whole, final)
    return (
        out_g.astype(jnp.bfloat16),
        out_u.astype(jnp.bfloat16),
        out_d.astype(jnp.bfloat16),
        weights,
    )


def solution(mesh):
    finer = Mesh(mesh.devices.reshape(8, 2, 2, 4, 2), ("dp_0", "dp_1", "dp_2", "mp_0", "mp_1"))
    placed = (
        P(MP, DP),
        P(MP, DP),
        P(MP, DP),
        P(MP, DP),
        P(DP, MP),
        P(DP, MP),
        P(MP, DP),
        P(),
        P(),
        P(),
    )
    return jax.shard_map(
        body,
        mesh=finer,
        in_specs=placed,
        out_specs=(P(DP, MP), P(DP, MP), P(MP, DP), P()),
        check_vma=False,
    )
```

profile of v0, /device:TPU:1, one launch (start us, length us, event | category | flops | bytes accessed | tf_op | source)
XLA Modules:
  0.0 287.9 jit_solution(6815766048710148342)
XLA Ops:
  0.6 0.8 pad_maximum_fusion.3
  1.5 24.4 %all_gather.6 = bf16[256,512]{1,0:T(8,128)(2,1)S(1)} all-gather(bf16[32,512]{1,0:T(8,128)(2,1)S(1)} %pad_maximum_fusion.3), channel_id=1, replica_groups=mesh['dp_0'=8,'dp_1'=2,'dp_2'=2,'mp_0'=4,'mp_1'=2] {'mp_0','mp_1'}, dimensions={0}, use_global_device_ids=true | all-gather | bytes 294912 | tf_op jit(solution)/shard_map/all_gather | solution.py:56
  25.9 1.6 fusion.46
  27.5 0.0 copy-start
  27.5 0.4 fusion.52
  27.9 0.8 copy-done
  28.7 0.4 fusion.54
  29.1 0.4 pad_maximum_fusion
  29.4 0.4 copy.26
  29.8 16.7 %all_to_all.43 = f32[2,16,8,5376]{3,2,1,0:T(8,128)} all-to-all(f32[2,16,8,5376]{3,2,1,0:T(8,128)S(1)} %bitcast.28), channel_id=1, replica_groups=mesh['dp_0'=8,'dp_1'=2,'dp_2'=2,'mp_0'=4,'mp_1'=2] {'dp_2'}, dimensions={0} | all-to-all | bytes 11010048 | tf_op jit(solution)/shard_map/all_to_all | solution.py:25
  46.5 3.2 %reduce_sum.95 = f32[16,8,5376]{2,1,0:T(8,128)S(1)} reduce(f32[2,16,8,5376]{3,2,1,0:T(8,128)} %all_to_all.43, f32[]{:T(128)} %constant.7.clone.1), dimensions={0}, to_apply=%region_1.0 | reduce | flops 688128 | bytes 8257540 | tf_op jit(solution)/shard_map/reduce_sum | solution.py:26
  49.7 75.3 %all_to_all.44 = f32[16,8,5376]{2,1,0:T(8,128)} all-to-all(f32[16,8,5376]{2,1,0:T(8,128)S(1)} %reduce_sum.95), channel_id=1, replica_groups=mesh['dp_0'=8,'dp_1'=2,'dp_2'=2,'mp_0'=4,'mp_1'=2] {'dp_0','dp_1'}, dimensions={0} | all-to-all | bytes 5505024 | tf_op jit(solution)/shard_map/all_to_all | solution.py:32
  125.0 1.9 reduce_sum.96
  127.0 0.0 copy-start.7
  127.0 1.2 broadcast_in_dim.57
  128.2 4.4 %all-to-all-start.2 = ((bf16[16,8,5376]{2,1,0:T(8,128)(2,1)}), bf16[16,8,5376]{2,1,0:T(8,128)(2,1)}, u32[]{:S(2)}, u32[]{:S(2)}) async-start(bf16[16,8,5376]{2,1,0:T(8,128)(2,1)} %broadcast_in_dim.57), calls=%async_computation.2 | async-start | bytes 2752512 | tf_op jit(solution)/shard_map/all_to_all | solution.py:37
  132.6 23.7 %all-gather = bf16[8,4,512]{2,1,0:T(4,128)(2,1)S(1)} all-gather(bf16[1,4,512]{2,1,0:T(4,128)(2,1)S(1)} %maximum_bitcast_fusion), channel_id=1, replica_groups=mesh['dp_0'=8,'dp_1'=2,'dp_2'=2,'mp_0'=4,'mp_1'=2] {'mp_0','mp_1'}, dimensions={0}, use_global_device_ids=true | all-gather | bytes 36864 | tf_op jit(solution)/shard_map/all_gather | solution.py:56
  156.4 0.1 select_reduce_fusion.2
  156.5 8.8 %all-to-all-done.2 = bf16[16,8,5376]{2,1,0:T(8,128)(2,1)} async-done(((bf16[16,8,5376]{2,1,0:T(8,128)(2,1)}), bf16[16,8,5376]{2,1,0:T(8,128)(2,1)}, u32[]{:S(2)}, u32[]{:S(2)}) %all-to-all-start.2) | async-done | bytes 1376288 | tf_op jit(solution)/shard_map/all_to_all | solution.py:37
  165.3 1.5 broadcast_in_dim.58
  166.8 11.0 %all_to_all.45 = bf16[2,16,8,5376]{3,2,1,0:T(8,128)(2,1)S(1)} all-to-all(bf16[2,16,8,5376]{3,2,1,0:T(8,128)(2,1)S(1)} %broadcast_in_dim.58), channel_id=1, replica_groups=mesh['dp_0'=8,'dp_1'=2,'dp_2'=2,'mp_0'=4,'mp_1'=2] {'dp_2'}, dimensions={0} | all-to-all | bytes 5505024 | tf_op jit(solution)/shard_map/all_to_all | solution.py:37
  177.8 0.2 copy.19
  178.0 0.7 fusion.9
  178.7 0.4 copy-done.1
  179.2 0.4 fusion.13
  179.5 0.8 copy-done.3
  180.3 0.4 fusion.15
  180.7 2.7 fusion.12
  183.4 1.8 pad_maximum_fusion.1
  185.2 2.3 reshape_reshape.14
  187.6 1.1 copy.27
  188.7 5.0 %all_to_all.46 = f32[2,16,1,5376]{3,1,2,0:T(8,128)} all-to-all(f32[2,16,1,5376]{3,1,2,0:T(8,128)S(1)} %bitcast.30), channel_id=1, replica_groups=mesh['dp_0'=8,'dp_1'=2,'dp_2'=2,'mp_0'=4,'mp_1'=2] {'dp_2'}, dimensions={0} | all-to-all | bytes 1376256 | tf_op jit(solution)/shard_map/all_to_all | solution.py:25
  193.8 1.2 reduce_sum.97
  195.0 0.2 reduce_sum.98
  195.2 20.5 %all_to_all.47 = f32[16,1,5376]{2,1,0:T(1,128)S(1)} all-to-all(f32[16,1,5376]{2,1,0:T(1,128)S(1)} %reduce_sum.98), channel_id=1, replica_groups=mesh['dp_0'=8,'dp_1'=2,'dp_2'=2,'mp_0'=4,'mp_1'=2] {'dp_0','dp_1'}, dimensions={0} | all-to-all | bytes 688128 | tf_op jit(solution)/shard_map/all_to_all | solution.py:32
  215.7 0.2 reduce_sum.99
  216.0 0.1 maximum_reduce_fusion
  216.1 0.2 broadcast_in_dim.59
  216.3 0.5 broadcast.46
  216.8 1.6 reduce.4
  218.4 0.7 reshape.22
  219.1 3.9 %all-to-all-start.6 = ((bf16[16,2,2688]{2,1,0:T(2,128)(2,1)}), bf16[16,2,2688]{2,1,0:T(2,128)(2,1)S(1)}, u32[]{:S(2)}, u32[]{:S(2)}) async-start(bf16[16,2,2688]{2,1,0:T(2,128)(2,1)} %reshape.22), calls=%async_computation.6 | async-start | bytes 344064 | tf_op jit(solution)/shard_map/all_to_all | solution.py:37
  223.0 10.3 %all-to-all-done.6 = bf16[16,2,2688]{2,1,0:T(2,128)(2,1)S(1)} async-done(((bf16[16,2,2688]{2,1,0:T(2,128)(2,1)}), bf16[16,2,2688]{2,1,0:T(2,128)(2,1)S(1)}, u32[]{:S(2)}, u32[]{:S(2)}) %all-to-all-start.6) | async-done | bytes 172064 | tf_op jit(solution)/shard_map/all_to_all | solution.py:37
  233.3 0.1 reshape.23
  233.5 6.2 %all_to_all.48 = bf16[2,16,1,5376]{3,1,2,0:T(8,128)(2,1)S(1)} all-to-all(bf16[2,16,1,5376]{3,1,2,0:T(8,128)(2,1)S(1)} %broadcast_in_dim.60), channel_id=1, replica_groups=mesh['dp_0'=8,'dp_1'=2,'dp_2'=2,'mp_0'=4,'mp_1'=2] {'dp_2'}, dimensions={0} | all-to-all | bytes 688128 | tf_op jit(solution)/shard_map/all_to_all | solution.py:37
  239.7 0.3 copy.21
  240.0 0.9 reshape_reshape.15
  240.9 1.7 convolution_convert_fusion.1
  242.5 0.4 convolution_multiply_fusion.2
  243.0 1.7 fusion.1
  244.7 2.5 fusion.11
  247.2 0.1 select_reduce_fusion.1
  247.3 10.8 %psum.35 = f32[8]{0:T(128)S(1)} all-reduce(f32[8]{0:T(128)S(1)} %select_reduce_fusion.1), channel_id=1, replica_groups=mesh['dp_0'=8,'dp_1'=2,'dp_2'=2,'mp_0'=4,'mp_1'=2] {'dp_0'}, use_global_device_ids=true, to_apply=%region_7.8 | all-reduce | flops 8 | bytes 64 | tf_op jit(solution)/shard_map/psum | solution.py:61
  258.1 5.3 %psum.36 = f32[8]{0:T(128)S(1)} all-reduce(f32[8]{0:T(128)S(1)} %psum.35), channel_id=1, replica_groups=mesh['dp_0'=8,'dp_1'=2,'dp_2'=2,'mp_0'=4,'mp_1'=2] {'dp_1'}, use_global_device_ids=true, to_apply=%region_8.9 | all-reduce | flops 8 | bytes 64 | tf_op jit(solution)/shard_map/psum | solution.py:61
  263.4 7.3 %psum.37 = f32[8]{0:T(128)S(1)} all-reduce(f32[8]{0:T(128)S(1)} %psum.36), channel_id=1, replica_groups=mesh['dp_0'=8,'dp_1'=2,'dp_2'=2,'mp_0'=4,'mp_1'=2] {'dp_2'}, use_global_device_ids=true, to_apply=%region_9.10 | all-reduce | flops 8 | bytes 64 | tf_op jit(solution)/shard_map/psum | solution.py:61
  270.7 6.2 %psum.38 = f32[8]{0:T(128)S(1)} all-reduce(f32[8]{0:T(128)S(1)} %psum.37), channel_id=1, replica_groups=mesh['dp_0'=8,'dp_1'=2,'dp_2'=2,'mp_0'=4,'mp_1'=2] {'mp_0'}, use_global_device_ids=true, to_apply=%region_10.11 | all-reduce | flops 8 | bytes 64 | tf_op jit(solution)/shard_map/psum | solution.py:61
  277.0 4.7 %psum.39 = f32[8]{0:T(128)S(1)} all-reduce(f32[8]{0:T(128)S(1)} %psum.38), channel_id=1, replica_groups=mesh['dp_0'=8,'dp_1'=2,'dp_2'=2,'mp_0'=4,'mp_1'=2] {'mp_1'}, use_global_device_ids=true, to_apply=%region_11.12 | all-reduce | flops 8 | bytes 64 | tf_op jit(solution)/shard_map/psum | solution.py:61
  281.7 0.6 multiply_reduce_fusion
  283.0 0.6 fusion.69
  283.6 0.6 multiply_divide_fusion
  284.3 0.1 select_reduce_fusion
  284.3 1.4 convolution_convert_fusion.2
  285.8 0.7 convolution_convert_fusion
  286.5 1.3 fusion.70
  (29 shorter events, 0.3 us)
Async XLA Ops:
  0.6 26.8 %copy-start.2 = (bf16[256,1792]{1,0:T(8,128)(2,1)S(1)}, bf16[256,1792]{1,0:T(8,128)(2,1)}, u32[]{:S(2)}) copy-start(bf16[256,1792]{1,0:T(8,128)(2,1)} %param.15) | copy-start | bytes 2752516
  27.5 1.2 copy-start
  127.0 5.6 %copy-start.7 = (bf16[4,256]{1,0:T(4,128)(2,1)S(1)}, bf16[4,256]{1,0:T(4,128)(2,1)}, u32[]{:S(2)}) copy-start(bf16[4,256]{1,0:T(4,128)(2,1)} %param.13) | copy-start | bytes 6148
  127.0 5.6 %copy-start.8 = (bf16[4,256]{1,0:T(4,128)(2,1)S(1)}, bf16[4,256]{1,0:T(4,128)(2,1)}, u32[]{:S(2)}) copy-start(bf16[4,256]{1,0:T(4,128)(2,1)} %param.12) | copy-start | bytes 6148
  127.0 29.4 %copy-start.6 = (s32[256]{0:T(256)S(1)}, s32[256]{0:T(256)}, u32[]{:S(2)}) copy-start(s32[256]{0:T(256)} %param.18) | copy-start | bytes 3076
  127.0 29.4 %copy-start.9 = (f32[8]{0:T(128)S(1)}, f32[8]{0:T(128)}, u32[]{:S(2)}) copy-start(f32[8]{0:T(128)} %param.17) | copy-start | bytes 100
  128.2 37.0 %all-to-all-start.2 = ((bf16[16,8,5376]{2,1,0:T(8,128)(2,1)}), bf16[16,8,5376]{2,1,0:T(8,128)(2,1)}, u32[]{:S(2)}, u32[]{:S(2)}) async-start(bf16[16,8,5376]{2,1,0:T(8,128)(2,1)} %broadcast_in_dim.57), calls=%async_computation.2 | async-start | bytes 2752512 | tf_op jit(solution)/shard_map/all_to_all | solution.py:37
  156.4 24.3 %copy-start.4 = (bf16[32,512]{1,0:T(8,128)(2,1)}, bf16[32,512]{1,0:T(8,128)(2,1)S(1)}, u32[]{:S(2)}) copy-start(bf16[32,512]{1,0:T(8,128)(2,1)S(1)} %reshape.20) | copy-start | bytes 98308
  178.0 1.2 copy-start.1
  179.2 1.2 copy-start.3
  195.0 28.0 %copy-start.11 = (s32[32]{0:T(128)S(1)}, s32[32]{0:T(128)}, u32[]{:S(2)}) copy-start(s32[32]{0:T(128)} %param.19) | copy-start | bytes 388
  219.1 14.2 %all-to-all-start.6 = ((bf16[16,2,2688]{2,1,0:T(2,128)(2,1)}), bf16[16,2,2688]{2,1,0:T(2,128)(2,1)S(1)}, u32[]{:S(2)}, u32[]{:S(2)}) async-start(bf16[16,2,2688]{2,1,0:T(2,128)(2,1)} %reshape.22), calls=%async_computation.6 | async-start | bytes 344064 | tf_op jit(solution)/shard_map/all_to_all | solution.py:37
  233.5 7.4 %copy-start.5 = (bf16[32,512]{1,0:T(8,128)(2,1)S(1)}, bf16[32,512]{1,0:T(8,128)(2,1)}, u32[]{:S(2)}) copy-start(bf16[32,512]{1,0:T(8,128)(2,1)} %copy-done.4) | copy-start | bytes 98308
  284.2 2.3 copy-start.10
where the time goes:
time: 291 us; the launch traced here: 288 us
  blocking collectives  217 us (75%)
  waiting for transfers between devices  19.1 us (7%)
  matrix products  15.1 us (5%)
  other arithmetic  13.5 us (5%)
  local copies, waits for them, and re-layouts  13.1 us (5%)
  starting transfers between devices  8.25 us (3%)
    all_to_all x2, blocking collectives, sum_in_two_steps(): return jnp.sum(lax.all_to_all(own, far, 0, 0, tiled=True), axis=0)  95.8 us
    all_gather x2, blocking collectives, side_by_side(): out = lax.all_gather(both, axis, axis=dim, tiled=True)  48.1 us
    psum x5, blocking collectives, over_axes(): return functools.reduce(lax.psum, axes, array)  34.4 us
    all_to_all x2, blocking collectives, sent_and_summed(): blocks = lax.all_to_all(split_up(array, dim, size), axis, 0, 0, tiled=True)  21.7 us
    all_to_all x2, waiting for transfers between devices, from_everyone(): return lax.all_to_all(copies, axis, split_axis=0, concat_axis=0, tiled=True)  19.1 us
    all_to_all x2, blocking collectives, from_everyone(): return lax.all_to_all(copies, axis, split_axis=0, concat_axis=0, tiled=True)  17.2 us
    all_to_all x2, starting transfers between devices, from_everyone(): return lax.all_to_all(copies, axis, split_axis=0, concat_axis=0, tiled=True)  8.25 us
    dot_general x3, matrix products, contract_width(): lax.dot_general(left, right, (((1,), (1,)), ((), ())), preferred_element_...  6.79 us
  transfers between devices with their start and end apart: 2, of which 2 were waited for; matrix products, arithmetic and copies ran while one was open for 0% of the time, Pallas kernels for 0%

commit v1 on v0

v1 whole, which is shorter than its diff:
```python
import jax
import jax.numpy as jnp
from jax import lax
from jax.experimental import pallas as pl
from jax.experimental.pallas import tpu as pltpu
from jax.sharding import PartitionSpec as P

MESH = pl.DeviceIdType.MESH
BF = jnp.bfloat16
F32 = jnp.float32

LEARN_RATE = 0.0003
NZ = 8
NM = 8
HB = 112
TOK = 256
W = 256
EX = 8


def nt(left, right):
    return lax.dot_general(left, right, (((1,), (1,)), ((), ())), preferred_element_type=F32)


def tn(left, right):
    return lax.dot_general(left, right, (((0,), (0,)), ((), ())), preferred_element_type=F32)


def comm_kernel(
    x_in, c_in, vx_in, vc_in, wg_in, wu_in, wd_in, sw, ids, mask,
    full_out, xs_out, wts_out,
    wraw, wt, wo, pk, vstage, xb, xo, va, vo, part, full,
    long_r_s, long_r_d, long_l_s, long_l_d, short_r_s, short_r_d, short_l_s, short_l_d,
    swap_s, swap_d, gram_s, gram_d, gram_x, gram_all, sc1, sc2, sc3, xt, xs,
    lsem, ssem, rsem, hsem,
):
    d = lax.axis_index("dp")
    m = lax.axis_index("mp")
    z = d // 4
    xh = (d // 2) % 2
    c = d % 2

    def dev(zz, xx, cc):
        return (zz * 4 + xx * 2 + cc, m)

    def zdev(step):
        return dev((z + step + NZ) % NZ, xh, c)

    def mdev(step):
        return (d, (m + step) % NM)

    other = dev(z, xh, 1 - c)
    across = dev(z, 1 - xh, c)
    diagonal = dev(z, 1 - xh, 1 - c)

    sends = []
    n_send = [0]

    def send(src, dst, rs, to):
        copy = pltpu.make_async_remote_copy(
            src_ref=src, dst_ref=dst, send_sem=ssem.at[n_send[0]], recv_sem=rsem.at[rs],
            device_id=to, device_id_type=MESH,
        )
        n_send[0] += 1
        copy.start()
        sends.append(copy)

    def got(dst, rs):
        pltpu.make_async_copy(dst, dst, rsem.at[rs]).wait()

    R_X, R_XO, R_W, R_RING, R_SWAP = 0, 8, 16, 24, 40
    R_GS, R_GX, R_GA, R_GC = 42, 50, 51, 59
    R_AR, R_AC, R_S1, R_S2, R_S3 = 60, 76, 84, 92, 100

    loads = [
        pltpu.make_async_copy(x_in, pk.at[0:32], lsem.at[0]),
        pltpu.make_async_copy(c_in, pk.at[32:64], lsem.at[1]),
        pltpu.make_async_copy(wg_in, wraw.at[0], lsem.at[2]),
        pltpu.make_async_copy(wu_in, wraw.at[1], lsem.at[3]),
        pltpu.make_async_copy(wd_in, wt.at[:, 2], lsem.at[4]),
    ]
    for copy in loads:
        copy.start()

    barrier = pltpu.get_barrier_semaphore()
    peers = [zdev(k) for k in range(1, NZ)] + [mdev(k) for k in range(1, NM)] + [other, across, diagonal]
    for peer in peers:
        pl.semaphore_signal(barrier, inc=1, device_id=peer, device_id_type=MESH)

    vstage[0:16] = jnp.zeros((16, W), F32)
    vstage[0:4] = vx_in[...].astype(F32)
    vstage[4:8] = vx_in[...].astype(F32)
    vstage[8:12] = vc_in[...].astype(F32)
    pk[64:80] = vstage[0:16].astype(BF)
    loads[0].wait()
    loads[1].wait()
    xb[m] = pk[...]
    pl.semaphore_wait(barrier, len(peers))

    for k in range(1, NM):
        send(pk, xb.at[m], R_X + m, mdev(k))
    send(pk, xo.at[m], R_XO + m, other)

    for w in range(2):
        loads[2 + w].wait()
        for i in range(14):
            block = wraw[w, :, 128 * i : 128 * (i + 1)].T
            at = 128 * i
            while at < 128 * (i + 1):
                b = at // HB
                end = min(128 * (i + 1), (b + 1) * HB)
                wt[b, w, at - b * HB : end - b * HB] = block[at - 128 * i : end - 128 * i]
                at = end
    loads[4].wait()
    for step in (4, 3, 5, 2, 6, 1, 7, 0):
        k = (z + step) % NZ
        send(wt.at[2 * k + 1 - c], wo.at[k], R_W + k, other)

    for k in range(1, NM):
        j = (m + NM - k) % NM
        got(xb.at[j], R_X + j)
        send(xb.at[j], xo.at[j], R_XO + j, other)
    for k in range(NM):
        j = (m + NM - k) % NM
        got(xo.at[j], R_XO + j)

    place = lax.broadcasted_iota(jnp.int32, (128, W), 0) % 16
    for src, dst in ((xb, va), (xo, vo)):
        rows = src[:, 64:80, :].reshape(128, W).astype(F32)
        for i in range(3):
            keep = jnp.logical_and(place >= 4 * i, place < 4 * i + 4)
            dst[i] = jnp.where(keep, rows, 0.0).astype(BF)

    def tokens(ref, first):
        return ref[:, 32 * first : 32 * first + 32, :].reshape(TOK, W)

    def partial_sums(k):
        got(wo.at[k], R_W + k)
        b = 2 * k + c
        val = jnp.zeros((HB, 128), F32)
        for i in range(3):
            first = 1 if i == 2 else 0
            total = nt(wt[b, i], tokens(xb, first)) + nt(wo[k, i], tokens(xo, first))
            part[k, i] = total[:, :128]
            part[k, 4 + i] = total[:, 128:]
            val = val + nt(wt[b, i], va[i]) + nt(wo[k, i], vo[i])
        part[k, 3] = val

    A, B = slice(0, 4), slice(4, 7)

    def at(step):
        return (z + step + NZ) % NZ

    RL, RS, LL, LS = R_RING, R_RING + 4, R_RING + 8, R_RING + 12

    def first(s_buf, d_buf, rows, rs, step, to):
        s_buf[0] = part[at(step), rows].astype(BF)
        send(s_buf.at[0], d_buf.at[0], rs, to)

    def onward(s_buf, d_buf, rows, rs, s, step, to):
        got(d_buf.at[s - 1], rs + s - 1)
        s_buf[s] = (part[at(step), rows] + d_buf[s - 1].astype(F32)).astype(BF)
        send(s_buf.at[s], d_buf.at[s], rs + s, to)

    right, left = zdev(1), zdev(-1)
    partial_sums(at(4))
    first(long_r_s, long_r_d, A, RL, 4, right)
    first(long_l_s, long_l_d, B, LL, 4, left)
    partial_sums(at(3))
    first(short_r_s, short_r_d, B, RS, 3, right)
    partial_sums(at(-3))
    first(short_l_s, short_l_d, A, LS, -3, left)

    def half(ref, first):
        return ref[pl.ds(4 * c, 4), 32 * first : 32 * first + 32, :].reshape(128, W)

    gram = nt(va[0], half(xb, 0)) + nt(vo[0], half(xo, 0)) + nt(va[2], half(xb, 1)) + nt(vo[2], half(xo, 1))
    gram_s[...] = gram.reshape(NZ, 16, 128)
    gram_d[z] = gram_s[z]
    for k in range(1, NZ):
        send(gram_s.at[at(k)], gram_d.at[z], R_GS + z, zdev(k))

    onward(long_r_s, long_r_d, A, RL, 1, 3, right)
    onward(long_l_s, long_l_d, B, LL, 1, -3, left)
    partial_sums(at(2))
    partial_sums(at(-2))
    onward(short_r_s, short_r_d, B, RS, 1, 2, right)
    onward(short_l_s, short_l_d, A, LS, 1, -2, left)

    for k in range(1, NZ):
        got(gram_d.at[at(k)], R_GS + at(k))
    gram_x[0] = jnp.sum(gram_d[...], axis=0)
    send(gram_x.at[0], gram_x.at[1], R_GX, across)

    onward(long_r_s, long_r_d, A, RL, 2, 2, right)
    onward(long_l_s, long_l_d, B, LL, 2, -2, left)
    partial_sums(at(1))
    partial_sums(at(-1))
    onward(short_r_s, short_r_d, B, RS, 2, 1, right)
    onward(short_l_s, short_l_d, A, LS, 2, -1, left)

    got(gram_x.at[1], R_GX)
    gram_all[c, z] = gram_x[0] + gram_x[1]
    for k in range(1, NZ):
        send(gram_all.at[c, z], gram_all.at[c, z], R_GA + z, zdev(k))

    onward(long_r_s, long_r_d, A, RL, 3, 1, right)
    onward(long_l_s, long_l_d, B, LL, 3, -1, left)
    partial_sums(z)

    for k in range(1, NZ):
        got(gram_all.at[c, at(k)], R_GA + at(k))
    send(gram_all.at[c], gram_all.at[c], R_GC, other)

    r_row = jnp.zeros((1, TOK), F32)
    for e in range(EX):
        r_row = r_row + jnp.where(ids[...] == e, sw[e], 0.0)
    for i in range(2):
        xt[i] = tokens(xb, i).T.astype(F32)

    got(short_r_d.at[2], RS + 2)
    got(long_l_d.at[3], LL + 3)
    own_b = part[z, B] + short_r_d[2].astype(F32) + long_l_d[3].astype(F32)
    part[z, B] = own_b
    swap_s[B] = own_b.astype(BF)
    send(swap_s.at[B], swap_d.at[B], R_SWAP + 1, across)
    got(short_l_d.at[2], LS + 2)
    got(long_r_d.at[3], RL + 3)
    own_a = part[z, A] + short_l_d[2].astype(F32) + long_r_d[3].astype(F32)
    part[z, A] = own_a
    swap_s[A] = own_a.astype(BF)
    send(swap_s.at[A], swap_d.at[A], R_SWAP, across)

    def block_terms(gate, up, back):
        sig = 1.0 / (1.0 + jnp.exp(-gate))
        act = gate * sig
        return act * up, back * up * sig * (1.0 + gate * (1.0 - sig)), back * act

    mine = 2 * z + c

    def ahead(lo, hi, s, block, sem, to):
        send(full.at[block, lo:hi], full.at[block, lo:hi], sem, to)

    AR, AL = R_AR, R_AR + 8
    got(swap_d.at[B], R_SWAP + 1)
    for h, lo in ((1, 4), (0, 0)):
        if h == 0:
            got(swap_d.at[A], R_SWAP)
        total = [part[z, lo + i] + swap_d[lo + i].astype(F32) for i in range(3)]
        hid, dg, du = block_terms(*total)
        full[mine, 3 * h] = hid.astype(BF)
        full[mine, 3 * h + 1] = dg.astype(BF)
        full[mine, 3 * h + 2] = du.astype(BF)
        send(full.at[mine, 3 * h : 3 * h + 3], full.at[mine, 3 * h : 3 * h + 3], AR + h, right)
        send(full.at[mine, 3 * h : 3 * h + 3], full.at[mine, 3 * h : 3 * h + 3], AL + h, left)
    send(full.at[mine], full.at[mine], R_AC + z, other)
    outs = []

    def flush(block, sem):
        copy = pltpu.make_async_copy(full.at[block], full_out.at[block], hsem.at[sem])
        copy.start()
        outs.append(copy)

    def arrived(step, base, towards, to):
        zz = at(-step) if towards > 0 else at(step)
        block = 2 * zz + c
        for h in (1, 0):
            if step == 4 and h == (1 if towards > 0 else 0):
                continue
            piece = full.at[block, 3 * h : 3 * h + 3]
            got(piece, base + (step - 1) * 2 + h)
            if step < 3 or (step == 3 and h == (0 if towards > 0 else 1)):
                send(piece, piece, base + step * 2 + h, to)
        return zz, block

    def step_of_gather(step):
        if step < 4:
            zr, br = arrived(step, AR, 1, right)
            zl, bl = arrived(step, AL, -1, left)
            send(full.at[br], full.at[br], R_AC + zr, other)
            send(full.at[bl], full.at[bl], R_AC + zl, other)
        else:
            arrived(step, AR, 1, right)
            zl, bl = arrived(step, AL, -1, left)
            send(full.at[bl], full.at[bl], R_AC + zl, other)

    got(gram_all.at[1 - c], R_GC)
    kt = jnp.concatenate([gram_all[0].reshape(128, 128), gram_all[1].reshape(128, 128)], axis=1)
    rk = (kt * r_row).astype(BF)
    hb, dgb, dub = [jnp.concatenate([full[mine, i], full[mine, 3 + i]], axis=1) for i in range(3)]
    val = part[z, 3] + swap_d[3].astype(F32)
    v_gate = val - LEARN_RATE * nt(dgb, rk)
    v_up = pltpu.roll(val, 124, 1) - LEARN_RATE * nt(dub, rk)
    v_back = pltpu.roll(val - LEARN_RATE * nt(hb, rk), 120, 1)
    lane = lax.broadcasted_iota(jnp.int32, (32, 128), 1)
    row = lax.broadcasted_iota(jnp.int32, (32, 128), 0)
    pick = jnp.logical_and(lane % 16 < 4, (lane // 16) * 4 + lane % 16 == row)
    mask_f = jnp.broadcast_to(mask[...].astype(F32), (16, 32)).astype(BF)
    mask_l = lax.dot_general(
        mask_f, jnp.where(pick, 1.0, 0.0).astype(BF), (((1,), (0,)), ((), ())), preferred_element_type=F32
    )[0:1]
    keep = jnp.broadcast_to(mask_l, (HB, 128)) > 0.5
    v_hid, v_dg, v_du = [jnp.where(keep, t, 0.0) for t in block_terms(v_gate, v_up, v_back)]
    inner = tn(v_dg.astype(BF), dgb) + tn(v_du.astype(BF), dub) + tn(pltpu.roll(v_hid, 8, 1).astype(BF), hb)
    token = jnp.sum(inner * kt, axis=0, keepdims=True)
    label = lax.broadcasted_iota(jnp.int32, (EX, TOK), 0)
    score = 0.5 * jnp.sum(jnp.where(ids[...] == label, token, 0.0), axis=1, keepdims=True)
    sc1[z] = jnp.broadcast_to(score, (EX, 128))
    for k in range(1, NZ):
        send(sc1.at[z], sc1.at[z], R_S1 + z, zdev(k))

    step_of_gather(1)
    for k in range(1, NZ):
        got(sc1.at[at(k)], R_S1 + at(k))
    sc2[m] = jnp.sum(sc1[...], axis=0)
    for k in range(1, NM):
        send(sc2.at[m], sc2.at[m], R_S2 + m, mdev(k))

    step_of_gather(2)
    for k in range(1, NM):
        j = (m + k) % NM
        got(sc2.at[j], R_S2 + j)
    slot = xh * 2 + c
    sc3[slot] = jnp.sum(sc2[...], axis=0)
    for to in (other, across, diagonal):
        send(sc3.at[slot], sc3.at[slot], R_S3 + slot, to)

    step_of_gather(3)
    for k in range(1, 4):
        j = (slot + k) % 4
        got(sc3.at[j], R_S3 + j)
    score = jnp.sum(sc3[...], axis=0)
    rms = jnp.sqrt(jnp.mean(score * score, axis=0, keepdims=True) + 1e-6)
    arg = score / (4.0 * rms)
    soft = jnp.maximum(arg, 0.0) + jnp.log(1.0 + jnp.exp(-jnp.abs(arg)))
    weights = EX * soft / jnp.sum(soft, axis=0, keepdims=True)
    diag = lax.broadcasted_iota(jnp.int32, (EX, 128), 0) == lax.broadcasted_iota(jnp.int32, (EX, 128), 1)
    wts_out[...] = jnp.sum(jnp.where(diag, weights, 0.0), axis=0, keepdims=True)[:, :EX]
    e_row = jnp.zeros((1, TOK), F32)
    for e in range(EX):
        e_row = e_row + jnp.where(ids[...] == e, weights[e : e + 1, 0:1], 0.0)
    for i in range(2):
        xs[i] = (xt[i] * e_row).astype(BF)
    copy = pltpu.make_async_copy(xs, xs_out, hsem.at[16])
    copy.start()
    outs.append(copy)

    step_of_gather(4)
    for k in range(NZ):
        flush(2 * at(k) + c, k)
    for k in range(NZ):
        block = 2 * at(k) + 1 - c
        got(full.at[block], R_AC + at(k))
        flush(block, 8 + k)
    for copy in sends:
        copy.wait_send()
    for copy in outs:
        copy.wait()


def grad_kernel(full, xs, gg, gu, gd):
    def rows(i):
        return jnp.concatenate(
            [full[:, i].reshape(8 * HB, 128), full[:, 3 + i].reshape(8 * HB, 128)], axis=1
        )

    gd[...] = nt(rows(0), xs[1]).astype(BF)
    gg[...] = nt(xs[0], rows(1)).astype(BF)
    gu[...] = nt(xs[0], rows(2)).astype(BF)


def body(train_x, train_cot, val_x, val_cot, w_gate, w_up, w_down, step_weights, example_ids, val_mask):
    hbm = pl.BlockSpec(memory_space=pl.ANY)
    vmem = pl.BlockSpec(memory_space=pltpu.VMEM)
    V = pltpu.VMEM
    full, xs, wts = pl.pallas_call(
        comm_kernel,
        out_shape=(
            jax.ShapeDtypeStruct((16, 6, HB, 128), BF),
            jax.ShapeDtypeStruct((2, W, TOK), BF),
            jax.ShapeDtypeStruct((1, EX), F32),
        ),
        in_specs=[hbm, hbm, vmem, vmem, hbm, hbm, hbm, pl.BlockSpec(memory_space=pltpu.SMEM), vmem, vmem],
        out_specs=(hbm, hbm, vmem),
        scratch_shapes=[
            V((2, W, 1792), BF),
            V((16, 3, HB, W), BF),
            V((NZ, 3, HB, W), BF),
            V((80, W), BF),
            V((16, W), F32),
            V((NM, 80, W), BF),
            V((NM, 80, W), BF),
            V((3, 128, W), BF),
            V((3, 128, W), BF),
            V((NZ, 7, HB, 128), F32),
            V((16, 6, HB, 128), BF),
            V((4, 4, HB, 128), BF),
            V((4, 4, HB, 128), BF),
            V((4, 3, HB, 128), BF),
            V((4, 3, HB, 128), BF),
            V((3, 3, HB, 128), BF),
            V((3, 3, HB, 128), BF),
            V((3, 4, HB, 128), BF),
            V((3, 4, HB, 128), BF),
            V((7, HB, 128), BF),
            V((7, HB, 128), BF),
            V((NZ, 16, 128), F32),
            V((NZ, 16, 128), F32),
            V((2, 16, 128), F32),
            V((2, NZ, 16, 128), F32),
            V((NZ, EX, 128), F32),
            V((NM, EX, 128), F32),
            V((4, EX, 128), F32),
            V((2, W, TOK), F32),
            V((2, W, TOK), BF),
            pltpu.SemaphoreType.DMA((5,)),
            pltpu.SemaphoreType.DMA((120,)),
            pltpu.SemaphoreType.DMA((104,)),
            pltpu.SemaphoreType.DMA((17,)),
        ],
        compiler_params=pltpu.CompilerParams(
            collective_id=0, has_side_effects=True, vmem_limit_bytes=40 * 1024 * 1024
        ),
        name="reduce_and_gather",
    )(
        train_x, train_cot, val_x, val_cot, w_gate, w_up, w_down.reshape(16, HB, W),
        step_weights, example_ids.reshape(1, TOK), val_mask.reshape(1, 32),
    )
    gg, gu, gd = pl.pallas_call(
        grad_kernel,
        grid=(2,),
        out_shape=(
            jax.ShapeDtypeStruct((W, 1792), BF),
            jax.ShapeDtypeStruct((W, 1792), BF),
            jax.ShapeDtypeStruct((1792, W), BF),
        ),
        in_specs=[
            pl.BlockSpec((8, 6, HB, 128), lambda i: (i, 0, 0, 0)),
            pl.BlockSpec((2, W, TOK), lambda i: (0, 0, 0)),
        ],
        out_specs=(
            pl.BlockSpec((W, 8 * HB), lambda i: (0, i)),
            pl.BlockSpec((W, 8 * HB), lambda i: (0, i)),
            pl.BlockSpec((8 * HB, W), lambda i: (i, 0)),
        ),
        compiler_params=pltpu.CompilerParams(vmem_limit_bytes=40 * 1024 * 1024),
        name="gradients",
    )(full, xs)
    return gg, gu, gd, wts.reshape(EX)


def solution(mesh):
    wide, tall = P("dp", "mp"), P("mp", "dp")
    return jax.shard_map(
        body,
        mesh=mesh,
        in_specs=(tall, tall, tall, tall, wide, wide, tall, P(), P(), P()),
        out_specs=(wide, wide, tall, P()),
        check_vma=False,
    )
```

time: 291 us -> 79.4 us (0.27)
  blocking collectives: 217 us -> 0 us
  Pallas kernels: 0 us -> 69.1 us
  waiting for transfers between devices: 19.1 us -> 0 us
  matrix products: 15.1 us -> 0 us
  other arithmetic: 13.5 us -> 0 us
  starting transfers between devices: 8.25 us -> 0 us
  local copies, waits for them, and re-layouts: 13.1 us -> 8.82 us
    all_to_all x6 -> x0, blocking collectives: 135 us -> none  [the longest x2 95.8 us: sum_in_two_steps(): return jnp.sum(lax.all_to_all(own, far, 0, 0, tiled=True), axis=0)]
    pallas_call x0 -> x2, Pallas kernels: none -> 69.1 us  [the longest x1 66.9 us: body(): pl.pallas_call(comm_kernel, out_shape=(jax.ShapeDtypeStruct((16, 6, HB, 1...]
    all_gather x2 -> x0, blocking collectives: 48.1 us -> none  [side_by_side(): out = lax.all_gather(both, axis, axis=dim, tiled=True)]
    psum x5 -> x0, blocking collectives: 34.4 us -> none  [over_axes(): return functools.reduce(lax.psum, axes, array)]
    all_to_all x2 -> x0, waiting for transfers between devices: 19.1 us -> none  [from_everyone(): return lax.all_to_all(copies, axis, split_axis=0, concat_axis=0, tiled=True)]
    dot_general x13 -> x0, matrix products: 15.1 us -> none  [the longest x3 6.79 us: contract_width(): lax.dot_general(left, right, (((1,), (1,)), ((), ())), preferred_element_...]
    all_to_all x2 -> x0, starting transfers between devices: 8.25 us -> none  [from_everyone(): return lax.all_to_all(copies, axis, split_axis=0, concat_axis=0, tiled=True)]
    reduce_sum x9 -> x0, other arithmetic: 8.03 us -> none  [the longest x2 4.38 us: sent_and_summed(): return jnp.sum(blocks, axis=0)]
  transfers between devices with their start and end apart: 2 -> 0, of which waited for: 2 -> 0; matrix products, arithmetic and copies ran while one was open for 0% -> 0% of each run, Pallas kernels for 0% -> 0%
where the time goes in v1:
time: 79.4 us; the launch traced here: 78.5 us
  Pallas kernels  69.1 us (87%)
  local copies, waits for them, and re-layouts  8.82 us (11%)
    pallas_call x1, Pallas kernels, body(): pl.pallas_call(comm_kernel, out_shape=(jax.ShapeDtypeStruct((16, 6, HB, 1...  66.9 us
    unnamed x21, local copies, waits for them, and re-layouts  8.82 us
    pallas_call x1, Pallas kernels, body(): pl.pallas_call(grad_kernel, grid=(2,), out_shape=(jax.ShapeDtypeStruct((W...  2.19 us

profile of v1, /device:TPU:1, one launch (start us, length us, event | category | flops | bytes accessed | tf_op | source)
XLA Modules:
  0.0 78.5 jit_solution(6454873074580358721)
XLA Ops:
  0.6 0.0 copy-start
  0.6 1.2 %copy-done = bf16[256,1792]{1,0:T(8,128)(2,1)S(1)} copy-done((bf16[256,1792]{1,0:T(8,128)(2,1)S(1)}, bf16[256,1792]{1,0:T(8,128)(2,1)}, u32[]{:S(2)}) %copy-start) | copy-done | bytes 917528
  1.8 0.0 copy-start.1
  1.8 1.2 %copy-done.1 = bf16[256,1792]{1,0:T(8,128)(2,1)S(1)} copy-done((bf16[256,1792]{1,0:T(8,128)(2,1)S(1)}, bf16[256,1792]{1,0:T(8,128)(2,1)}, u32[]{:S(2)}) %copy-start.1) | copy-done | bytes 917528
  3.0 0.0 copy-start.2
  3.0 1.2 %copy-done.2 = bf16[1792,256]{1,0:T(8,128)(2,1)S(1)} copy-done((bf16[1792,256]{1,0:T(8,128)(2,1)S(1)}, bf16[1792,256]{1,0:T(8,128)(2,1)}, u32[]{:S(2)}) %copy-start.2) | copy-done | bytes 917528
  4.2 0.0 copy-start.3
  4.2 0.7 copy-done.3
  4.9 0.0 copy-start.4
  4.9 0.7 copy-done.4
  5.6 0.0 copy-start.5
  5.6 0.7 copy-done.5
  6.3 0.0 copy-start.6
  6.3 0.7 copy-done.6
  7.0 0.0 copy-start.7
  7.0 0.7 copy-done.7
  7.7 0.0 copy-start.8
  7.7 0.7 copy-done.8
  8.3 0.0 copy-start.9
  8.3 0.7 copy-done.9
  9.0 66.9 %reduce_and_gather.1 = (bf16[16,6,112,128]{3,2,1,0:T(8,128)(2,1)S(1)}, bf16[2,256,256]{2,1,0:T(8,128)(2,1)S(1)}, f32[1,8]{1,0:T(1,128)S(1)}) custom-call(bf16[32,256]{1,0:T(8,128)(2,1)S(1)} %copy-done.3, bf16[32,256]{1,0:T(8,128)(2,1)S(1)} %copy-done.4, bf16[4,256]{1,0:T(4,128)(2,1)S(1)} %copy-done.5, bf16[4,256]{1,0:T(4,128)(2,1)S(1)} %copy-done.6, ...), custom_call_target="tpu_custom_call" | custom-call | tf_op jit(solution)/shard_map/reduce_and_gather/pallas_call | solution.py:376
  75.8 2.2 %gradients.1 = (bf16[256,1792]{1,0:T(8,128)(2,1)}, bf16[256,1792]{1,0:T(8,128)(2,1)}, bf16[1792,256]{1,0:T(8,128)(2,1)}) custom-call(bf16[16,6,112,128]{3,2,1,0:T(8,128)(2,1)S(1)} %get-tuple-element.10.full, bf16[2,256,256]{2,1,0:T(8,128)(2,1)S(1)} %get-tuple-element.11.xs), custom_call_target="tpu_custom_call" | custom-call | tf_op jit(solution)/shard_map/gradients/pallas_call | solution.py:429
  78.0 0.5 copy.15
Async XLA Ops:
  0.6 1.2 %copy-start = (bf16[256,1792]{1,0:T(8,128)(2,1)S(1)}, bf16[256,1792]{1,0:T(8,128)(2,1)}, u32[]{:S(2)}) copy-start(bf16[256,1792]{1,0:T(8,128)(2,1)} %wg_in.1) | copy-start | bytes 2752516
  1.8 1.2 %copy-start.1 = (bf16[256,1792]{1,0:T(8,128)(2,1)S(1)}, bf16[256,1792]{1,0:T(8,128)(2,1)}, u32[]{:S(2)}) copy-start(bf16[256,1792]{1,0:T(8,128)(2,1)} %wu_in.1) | copy-start | bytes 2752516
  3.0 1.2 %copy-start.2 = (bf16[1792,256]{1,0:T(8,128)(2,1)S(1)}, bf16[1792,256]{1,0:T(8,128)(2,1)}, u32[]{:S(2)}) copy-start(bf16[1792,256]{1,0:T(8,128)(2,1)} %param.16) | copy-start | bytes 2752516
  4.2 0.7 copy-start.3
  4.9 0.7 copy-start.4
  5.6 0.7 copy-start.5
  6.3 0.7 copy-start.6
  7.0 0.7 copy-start.7
  7.7 0.7 copy-start.8
  8.3 0.7 copy-start.9

commit v2 on v1

v2 whole, which is shorter than its diff:
```python
import jax
import jax.numpy as jnp
from jax import lax
from jax.experimental import pallas as pl
from jax.experimental.pallas import tpu as pltpu
from jax.sharding import PartitionSpec as P

MESH = pl.DeviceIdType.MESH
BF = jnp.bfloat16
F32 = jnp.float32

LEARN_RATE = 0.0003
NZ = 8
NM = 8
HB = 112
TOK = 256
W = 256
EX = 8


def nt(left, right):
    return lax.dot_general(left, right, (((1,), (1,)), ((), ())), preferred_element_type=F32)


def tn(left, right):
    return lax.dot_general(left, right, (((0,), (0,)), ((), ())), preferred_element_type=F32)


def comm_kernel(
    x_in, c_in, vx_in, vc_in, wg_in, wu_in, wd_in, sw_in, ids_in, mask_in,
    full, xs_out, wts_out,
    sw, ids, mask, vraw, wraw, wt, wo, pk, vstage, xb, xo, va, vo, part, own,
    ring_s, ring_d, swap_p, swap_d, gram_s, gram_d, gram_x, gram_all, sc1, sc2, xt, xs,
    lsem, ssem, rsem, hsem,
):
    d = lax.axis_index("dp")
    m = lax.axis_index("mp")
    z = d // 4
    xh = (d // 2) % 2
    c = d % 2
    slot = z * 2 + c

    def dev(zz, xx, cc):
        return (zz * 4 + xx * 2 + cc, m)

    def at(step):
        return (z + step + NZ) % NZ

    def zdev(step):
        return dev(at(step), xh, c)

    def mdev(step):
        return (d, (m + step) % NM)

    def pdev(step):
        j = (slot + step) % 16
        return dev(j // 2, xh, j % 2)

    other = dev(z, xh, 1 - c)
    across = dev(z, 1 - xh, c)
    right, left = zdev(1), zdev(-1)

    sends = []

    def send(src, dst, rs, to):
        copy = pltpu.make_async_remote_copy(
            src_ref=src, dst_ref=dst, send_sem=ssem.at[len(sends)], recv_sem=rsem.at[rs],
            device_id=to, device_id_type=MESH,
        )
        copy.start()
        sends.append(copy)

    def got(dst, rs):
        pltpu.make_async_copy(dst, dst, rsem.at[rs]).wait()

    R_X, R_XO, R_W, R_RING = 0, 8, 16, 24
    R_P, R_SHORT, R_LONG = 80, 81, 88
    R_GS, R_GX, R_GA, R_GC = 96, 104, 105, 113
    R_A, R_AC, R_S1, R_S2 = 114, 162, 171, 187

    loads = [
        pltpu.make_async_copy(x_in, pk.at[0:32], lsem.at[0]),
        pltpu.make_async_copy(c_in, pk.at[32:64], lsem.at[1]),
        pltpu.make_async_copy(wg_in, wraw.at[0], lsem.at[2]),
        pltpu.make_async_copy(wu_in, wraw.at[1], lsem.at[3]),
        pltpu.make_async_copy(vx_in, vraw.at[0], lsem.at[4]),
        pltpu.make_async_copy(vc_in, vraw.at[1], lsem.at[5]),
        pltpu.make_async_copy(wd_in.at[:, 0], wt.at[0, :, 2], lsem.at[6]),
        pltpu.make_async_copy(wd_in.at[:, 1], wt.at[1, :, 2], lsem.at[7]),
        pltpu.make_async_copy(sw_in, sw, lsem.at[8]),
        pltpu.make_async_copy(ids_in, ids, lsem.at[9]),
        pltpu.make_async_copy(mask_in, mask, lsem.at[10]),
    ]
    for copy in loads:
        copy.start()

    barrier = pltpu.get_barrier_semaphore()
    peers = [mdev(k) for k in range(1, NM)] + [across] + [pdev(k) for k in range(1, 16)]
    for peer in peers:
        pl.semaphore_signal(barrier, inc=1, device_id=peer, device_id_type=MESH)

    vstage[0:16] = jnp.zeros((16, W), F32)
    loads[4].wait()
    loads[5].wait()
    vstage[0:4] = vraw[0].astype(F32)
    vstage[4:8] = vraw[0].astype(F32)
    vstage[8:12] = vraw[1].astype(F32)
    pk[64:80] = vstage[0:16].astype(BF)
    loads[0].wait()
    loads[1].wait()
    xb[m] = pk[...]
    pl.semaphore_wait(barrier, len(peers))

    for k in range(1, NM):
        send(pk, xb.at[m], R_X + m, mdev(k))
    send(pk, xo.at[m], R_XO + m, other)

    for w in range(2):
        loads[2 + w].wait()
        for i in range(14):
            block = wraw[w, :, 128 * i : 128 * (i + 1)].T
            row = 128 * i
            while row < 128 * (i + 1):
                b = row // HB
                end = min(128 * (i + 1), (b + 1) * HB)
                wt[b % 2, b // 2, w, row - b * HB : end - b * HB] = block[row - 128 * i : end - 128 * i]
                row = end
    loads[6].wait()
    loads[7].wait()
    for step in (4, 3, 5, 2, 6, 1, 7, 0):
        send(wt.at[1 - c, at(step)], wo.at[at(step)], R_W + at(step), other)

    for k in range(1, NM):
        j = (m + NM - k) % NM
        got(xb.at[j], R_X + j)
        send(xb.at[j], xo.at[j], R_XO + j, other)
    for k in range(NM):
        j = (m + NM - k) % NM
        got(xo.at[j], R_XO + j)

    place = lax.broadcasted_iota(jnp.int32, (128, W), 0) % 16
    for src, dst in ((xb, va), (xo, vo)):
        rows = src[:, 64:80, :].reshape(128, W).astype(F32)
        for i in range(3):
            keep = jnp.logical_and(place >= 4 * i, place < 4 * i + 4)
            dst[i] = jnp.where(keep, rows, 0.0).astype(BF)

    def tokens(ref, first):
        return ref[:, 32 * first : 32 * first + 32, :].reshape(TOK, W)

    A, B = (0, 1, 2, 3), (4, 5, 6)
    RIGHT, LEFT = 0, 1
    to_dev = (right, left)

    def first(way, slab, value):
        ring_s[way, 0, slab] = value.astype(BF)
        send(ring_s.at[way, 0, slab], ring_d.at[way, 0, slab], R_RING + way * 28 + slab, to_dev[way])

    def arrived(way, s, slab):
        got(ring_d.at[way, s - 1, slab], R_RING + (way * 4 + s - 1) * 7 + slab)

    def onward(way, s, slab, step):
        arrived(way, s, slab)
        value = part[at(step), slab] + ring_d[way, s - 1, slab].astype(F32)
        ring_s[way, s, slab] = value.astype(BF)
        send(
            ring_s.at[way, s, slab], ring_d.at[way, s, slab],
            R_RING + (way * 4 + s) * 7 + slab, to_dev[way],
        )

    far = at(4)
    got(wo.at[far], R_W + far)
    for i in range(3):
        which = 1 if i == 2 else 0
        total = nt(wt[c, far, i], tokens(xb, which)) + nt(wo[far, i], tokens(xo, which))
        first(RIGHT, i, total[:, :128])
        first(LEFT, 4 + i, total[:, 128:])
    val = jnp.zeros((HB, 128), F32)
    for i in range(3):
        val = val + nt(wt[c, far, i], va[i]) + nt(wo[far, i], vo[i])
    first(RIGHT, 3, val)

    for k in range(1, NZ):
        got(wo.at[at(4 + k)], R_W + at(4 + k))
    val = jnp.zeros((NZ * HB, 128), F32)
    for i in range(3):
        which = 1 if i == 2 else 0
        lhs, lho = wt[c, :, i].reshape(NZ * HB, W), wo[:, i].reshape(NZ * HB, W)
        total = nt(lhs, tokens(xb, which)) + nt(lho, tokens(xo, which))
        part[:, i] = total[:, :128].reshape(NZ, HB, 128)
        part[:, 4 + i] = total[:, 128:].reshape(NZ, HB, 128)
        first(LEFT, i, part[at(-3), i])
        first(RIGHT, 4 + i, part[at(3), 4 + i])
        val = val + nt(lhs, va[i]) + nt(lho, vo[i])
    part[:, 3] = val.reshape(NZ, HB, 128)
    first(LEFT, 3, part[at(-3), 3])
    send(part.at[z], swap_p, R_P, across)

    def both_long(s):
        for i in range(4):
            onward(RIGHT, s, A[i], 4 - s)
            if i < 3:
                onward(LEFT, s, B[i], s - 4)

    def both_short(s):
        for i in range(4):
            if i < 3:
                onward(RIGHT, s, B[i], 3 - s)
            onward(LEFT, s, A[i], s - 3)

    def half(ref, which):
        return ref[pl.ds(4 * c, 4), 32 * which : 32 * which + 32, :].reshape(128, W)

    gram = nt(va[0], half(xb, 0)) + nt(vo[0], half(xo, 0)) + nt(va[2], half(xb, 1)) + nt(vo[2], half(xo, 1))
    gram_s[...] = gram.reshape(NZ, 16, 128)
    gram_d[z] = gram_s[z]
    for k in range(1, NZ):
        send(gram_s.at[at(k)], gram_d.at[z], R_GS + z, zdev(k))

    both_long(1)
    both_short(1)
    for copy in loads[8:]:
        copy.wait()
    for k in range(1, NZ):
        got(gram_d.at[at(k)], R_GS + at(k))
    gram_x[0] = jnp.sum(gram_d[...], axis=0)
    send(gram_x.at[0], gram_x.at[1], R_GX, across)
    both_long(2)
    both_short(2)
    got(gram_x.at[1], R_GX)
    gram_all[c, z] = gram_x[0] + gram_x[1]
    for k in range(1, NZ):
        send(gram_all.at[c, z], gram_all.at[c, z], R_GA + z, zdev(k))
    both_long(3)

    def pass_on(way, s, slab, dst, rs):
        arrived(way, s, slab)
        send(ring_d.at[way, s - 1, slab], swap_d.at[dst, slab], rs + slab, across)

    for i in range(4):
        if i < 3:
            pass_on(RIGHT, 3, B[i], 0, R_SHORT)
        pass_on(LEFT, 3, A[i], 0, R_SHORT)
    r_row = jnp.zeros((1, TOK), F32)
    for e in range(EX):
        r_row = r_row + jnp.where(ids[...] == e, sw[e], 0.0)
    for i in range(2):
        xt[i] = tokens(xb, i).T.astype(F32)
    for k in range(1, NZ):
        got(gram_all.at[c, at(k)], R_GA + at(k))
    send(gram_all.at[c], gram_all.at[c], R_GC, other)
    got(swap_p, R_P)
    for i in range(4):
        pass_on(RIGHT, 4, A[i], 1, R_LONG)
        if i < 3:
            pass_on(LEFT, 4, B[i], 1, R_LONG)

    def whole(slab):
        way = RIGHT if slab < 4 else LEFT
        mine_ = part[z, slab] + ring_d[1 - way, 2, slab].astype(F32) + ring_d[way, 3, slab].astype(F32)
        got(swap_d.at[0, slab], R_SHORT + slab)
        got(swap_d.at[1, slab], R_LONG + slab)
        theirs = swap_p[slab] + swap_d[0, slab].astype(F32) + swap_d[1, slab].astype(F32)
        return mine_ + theirs

    def block_terms(gate, up, back):
        sig = 1.0 / (1.0 + jnp.exp(-gate))
        act = gate * sig
        return act * up, back * up * sig * (1.0 + gate * (1.0 - sig)), back * act

    def gather(src, block, way, step, slab):
        send(
            src, full.at[block, slab], R_A + (way * 4 + step - 1) * 6 + slab, to_dev[way]
        )

    for h in range(2):
        terms = block_terms(*[whole(4 * h + i) for i in range(3)])
        for i in range(3):
            own[3 * h + i] = terms[i].astype(BF)
            gather(own.at[3 * h + i], slot, RIGHT, 1, 3 * h + i)
            gather(own.at[3 * h + i], slot, LEFT, 1, 3 * h + i)
    send(own, full.at[slot], R_AC + z, other)
    outs = [pltpu.make_async_copy(own, full.at[slot], hsem.at[0])]
    outs[0].start()

    def step_of_gather(step):
        blocks = [2 * at(-step) + c, 2 * at(step) + c]
        for i in range(6):
            for way in (RIGHT, LEFT):
                if step == 4 and i // 3 != way:
                    continue
                got(full.at[blocks[way], i], R_A + (way * 4 + step - 1) * 6 + i)
                if step < 3 or (step == 3 and i // 3 == way):
                    gather(full.at[blocks[way], i], blocks[way], way, step + 1, i)
        if step < 4:
            for way, zz in ((RIGHT, at(-step)), (LEFT, at(step))):
                send(full.at[blocks[way]], full.at[blocks[way]], R_AC + zz, other)
        else:
            send(full.at[blocks[0]], full.at[blocks[0]], R_AC + at(4), other)

    got(gram_all.at[1 - c], R_GC)
    kt = jnp.concatenate([gram_all[0].reshape(128, 128), gram_all[1].reshape(128, 128)], axis=1)
    rk = (kt * r_row).astype(BF)
    hb, dgb, dub = [jnp.concatenate([own[i], own[3 + i]], axis=1) for i in range(3)]
    val = whole(3)
    v_gate = val - LEARN_RATE * nt(dgb, rk)
    v_up = pltpu.roll(val, 124, 1) - LEARN_RATE * nt(dub, rk)
    v_back = pltpu.roll(val - LEARN_RATE * nt(hb, rk), 120, 1)
    lane = lax.broadcasted_iota(jnp.int32, (32, 128), 1)
    row = lax.broadcasted_iota(jnp.int32, (32, 128), 0)
    pick = jnp.logical_and(lane % 16 < 4, (lane // 16) * 4 + lane % 16 == row)
    mask_f = jnp.broadcast_to(mask[...].astype(F32), (16, 32)).astype(BF)
    mask_l = lax.dot_general(
        mask_f, jnp.where(pick, 1.0, 0.0).astype(BF), (((1,), (0,)), ((), ())), preferred_element_type=F32
    )[0:1]
    keep = jnp.broadcast_to(mask_l, (HB, 128)) > 0.5
    v_hid, v_dg, v_du = [jnp.where(keep, t, 0.0) for t in block_terms(v_gate, v_up, v_back)]
    inner = tn(v_dg.astype(BF), dgb) + tn(v_du.astype(BF), dub) + tn(pltpu.roll(v_hid, 8, 1).astype(BF), hb)
    token = jnp.sum(inner * kt, axis=0, keepdims=True)
    label = lax.broadcasted_iota(jnp.int32, (EX, TOK), 0)
    score = jnp.sum(jnp.where(ids[...] == label, token, 0.0), axis=1, keepdims=True)
    sc1[slot] = jnp.broadcast_to(score, (EX, 128))
    for k in range(1, 16):
        send(sc1.at[slot], sc1.at[slot], R_S1 + slot, pdev(k))

    step_of_gather(1)
    step_of_gather(2)
    for k in range(1, 16):
        j = (slot + k) % 16
        got(sc1.at[j], R_S1 + j)
    sc2[m] = jnp.sum(sc1[...], axis=0)
    for k in range(1, NM):
        send(sc2.at[m], sc2.at[m], R_S2 + m, mdev(k))

    step_of_gather(3)
    for k in range(1, NM):
        j = (m + k) % NM
        got(sc2.at[j], R_S2 + j)
    score = jnp.sum(sc2[...], axis=0)
    rms = jnp.sqrt(jnp.mean(score * score, axis=0, keepdims=True) + 1e-6)
    arg = score / (4.0 * rms)
    soft = jnp.maximum(arg, 0.0) + jnp.log(1.0 + jnp.exp(-jnp.abs(arg)))
    weights = EX * soft / jnp.sum(soft, axis=0, keepdims=True)
    diag = lax.broadcasted_iota(jnp.int32, (EX, 128), 0) == lax.broadcasted_iota(jnp.int32, (EX, 128), 1)
    wts_out[...] = jnp.sum(jnp.where(diag, weights, 0.0), axis=0, keepdims=True)[:, :EX]
    e_row = jnp.zeros((1, TOK), F32)
    for e in range(EX):
        e_row = e_row + jnp.where(ids[...] == e, weights[e : e + 1, 0:1], 0.0)
    for i in range(2):
        xs[i] = (xt[i] * e_row).astype(BF)
    copy = pltpu.make_async_copy(xs, xs_out, hsem.at[1])
    copy.start()
    outs.append(copy)

    step_of_gather(4)
    for k in range(NZ):
        got(full.at[2 * at(k) + 1 - c], R_AC + at(k))
    for copy in sends:
        copy.wait_send()
    for copy in outs:
        copy.wait()


def grad_kernel(full, xs, wts, gg, gu, gd, out):
    def rows(i):
        return jnp.concatenate(
            [full[:, i].reshape(8 * HB, 128), full[:, 3 + i].reshape(8 * HB, 128)], axis=1
        )

    out[...] = wts[...]
    gd[...] = nt(rows(0), xs[1]).astype(BF)
    gg[...] = nt(xs[0], rows(1)).astype(BF)
    gu[...] = nt(xs[0], rows(2)).astype(BF)


def body(train_x, train_cot, val_x, val_cot, w_gate, w_up, w_down, step_weights, example_ids, val_mask):
    hbm = pl.BlockSpec(memory_space=pltpu.HBM)
    free = pl.BlockSpec(memory_space=pl.ANY)
    vmem = pl.BlockSpec(memory_space=pltpu.VMEM)
    V = pltpu.VMEM
    full, xs, wts = pl.pallas_call(
        comm_kernel,
        out_shape=(
            jax.ShapeDtypeStruct((16, 6, HB, 128), BF),
            jax.ShapeDtypeStruct((2, W, TOK), BF),
            jax.ShapeDtypeStruct((1, EX), F32),
        ),
        in_specs=[hbm] * 10,
        out_specs=(free, free, vmem),
        scratch_shapes=[
            pltpu.SMEM((EX,), F32),
            V((1, TOK), jnp.int32),
            V((1, 32), jnp.int32),
            V((2, 4, W), BF),
            V((2, W, 1792), BF),
            V((2, NZ, 3, HB, W), BF),
            V((NZ, 3, HB, W), BF),
            V((80, W), BF),
            V((16, W), F32),
            V((NM, 80, W), BF),
            V((NM, 80, W), BF),
            V((3, 128, W), BF),
            V((3, 128, W), BF),
            V((NZ, 7, HB, 128), F32),
            V((6, HB, 128), BF),
            V((2, 4, 7, HB, 128), BF),
            V((2, 4, 7, HB, 128), BF),
            V((7, HB, 128), F32),
            V((2, 7, HB, 128), BF),
            V((NZ, 16, 128), F32),
            V((NZ, 16, 128), F32),
            V((2, 16, 128), F32),
            V((2, NZ, 16, 128), F32),
            V((16, EX, 128), F32),
            V((NM, EX, 128), F32),
            V((2, W, TOK), F32),
            V((2, W, TOK), BF),
            pltpu.SemaphoreType.DMA((11,)),
            pltpu.SemaphoreType.DMA((200,)),
            pltpu.SemaphoreType.DMA((195,)),
            pltpu.SemaphoreType.DMA((2,)),
        ],
        compiler_params=pltpu.CompilerParams(
            collective_id=0, has_side_effects=True, vmem_limit_bytes=40 * 1024 * 1024
        ),
        name="reduce_and_gather",
    )(
        *[
            pltpu.with_memory_space_constraint(a, pltpu.HBM)
            for a in (
                train_x, train_cot, val_x, val_cot, w_gate, w_up, w_down.reshape(NZ, 2, HB, W),
                step_weights, example_ids.reshape(1, TOK), val_mask.reshape(1, 32),
            )
        ]
    )
    gg, gu, gd, out = pl.pallas_call(
        grad_kernel,
        grid=(2,),
        out_shape=(
            jax.ShapeDtypeStruct((W, 1792), BF),
            jax.ShapeDtypeStruct((W, 1792), BF),
            jax.ShapeDtypeStruct((1792, W), BF),
            jax.ShapeDtypeStruct((1, EX), F32),
        ),
        in_specs=[
            pl.BlockSpec((8, 6, HB, 128), lambda i: (i, 0, 0, 0)),
            pl.BlockSpec((2, W, TOK), lambda i: (0, 0, 0)),
            pl.BlockSpec((1, EX), lambda i: (0, 0)),
        ],
        out_specs=(
            pl.BlockSpec((W, 8 * HB), lambda i: (0, i)),
            pl.BlockSpec((W, 8 * HB), lambda i: (0, i)),
            pl.BlockSpec((8 * HB, W), lambda i: (i, 0)),
            pl.BlockSpec((1, EX), lambda i: (0, 0)),
        ),
        compiler_params=pltpu.CompilerParams(vmem_limit_bytes=40 * 1024 * 1024),
        name="gradients",
    )(full, xs, wts)
    return gg, gu, gd, out.reshape(EX)


def solution(mesh):
    wide, tall = P("dp", "mp"), P("mp", "dp")
    return jax.shard_map(
        body,
        mesh=mesh,
        in_specs=(tall, tall, tall, tall, wide, wide, tall, P(), P(), P()),
        out_specs=(wide, wide, tall, P()),
        check_vma=False,
    )
```

time: 79.4 us -> 70 us (0.88)
  local copies, waits for them, and re-layouts: 8.82 us -> 0 us
    unnamed x21 -> x0, local copies, waits for them, and re-layouts: 8.82 us -> none
where the time goes in v2:
time: 70 us; the launch traced here: 69.9 us
  Pallas kernels  69.3 us (99%)
    pallas_call x1, Pallas kernels, body(): pl.pallas_call(comm_kernel, out_shape=(jax.ShapeDtypeStruct((16, 6, HB, 1...  67.1 us
    pallas_call x1, Pallas kernels, body(): pl.pallas_call(grad_kernel, grid=(2,), out_shape=(jax.ShapeDtypeStruct((W...  2.18 us

profile of v2, /device:TPU:1, one launch (start us, length us, event | category | flops | bytes accessed | tf_op | source)
XLA Modules:
  0.0 69.9 jit_solution(8164243689688613161)
XLA Ops:
  0.6 67.1 %reduce_and_gather.1 = (bf16[16,6,112,128]{3,2,1,0:T(8,128)(2,1)S(1)}, bf16[2,256,256]{2,1,0:T(8,128)(2,1)S(1)}, f32[1,8]{1,0:T(1,128)S(1)}) custom-call(bf16[32,256]{1,0:T(8,128)(2,1)} %x_in.1, bf16[32,256]{1,0:T(8,128)(2,1)} %c_in.1, bf16[4,256]{1,0:T(4,128)(2,1)} %vx_in.1, bf16[4,256]{1,0:T(4,128)(2,1)} %vc_in.1, bf16[256,1792]{1,0:T(8,128)(2,1)} %wg_in.1, ...), custom_call_target="tpu_custom_call" | custom-call | tf_op jit(solution)/shard_map/reduce_and_gather/pallas_call | solution.py:381
  67.7 2.2 %gradients.1 = (bf16[256,1792]{1,0:T(8,128)(2,1)}, bf16[256,1792]{1,0:T(8,128)(2,1)}, bf16[1792,256]{1,0:T(8,128)(2,1)}, f32[1,8]{1,0:T(1,128)}) custom-call(bf16[16,6,112,128]{3,2,1,0:T(8,128)(2,1)S(1)} %get-tuple-element.11.full, bf16[2,256,256]{2,1,0:T(8,128)(2,1)S(1)} %get-tuple-element.12.xs, f32[1,8]{1,0:T(1,128)S(1)} %get-tuple-element.13.wts), custom_call_target="tpu_custom_call" | custom-call | tf_op jit(solution)/shard_map/gradients/pallas_call | solution.py:436

commit v3 on v2

--- a/solution.py
+++ b/solution.py
@@ -29,8 +29,9 @@
 def comm_kernel(
     x_in, c_in, vx_in, vc_in, wg_in, wu_in, wd_in, sw_in, ids_in, mask_in,
     full, xs_out, wts_out,
-    sw, ids, mask, vraw, wraw, wt, wo, pk, vstage, xb, xo, va, vo, part, own,
-    ring_s, ring_d, swap_p, swap_d, gram_s, gram_d, gram_x, gram_all, sc1, sc2, xt, xs,
+    sw, ids, mask, vraw, wraw, wt, wo, pk, vstage, xb, xo, va, vo, part, vpart, own,
+    pair_s, pair_d, ring_s, ring_d, last_s, last_d, swap_p, swap_d,
+    gram_s, gram_d, gram_x, gram_all, sc1, sc2, sc3, xt, xs,
     lsem, ssem, rsem, hsem,
 ):
     d = lax.axis_index("dp")
@@ -52,10 +53,6 @@
     def mdev(step):
         return (d, (m + step) % NM)
 
-    def pdev(step):
-        j = (slot + step) % 16
-        return dev(j // 2, xh, j % 2)
-
     other = dev(z, xh, 1 - c)
     across = dev(z, 1 - xh, c)
     right, left = zdev(1), zdev(-1)
@@ -73,10 +70,11 @@
     def got(dst, rs):
         pltpu.make_async_copy(dst, dst, rsem.at[rs]).wait()
 
-    R_X, R_XO, R_W, R_RING = 0, 8, 16, 24
-    R_P, R_SHORT, R_LONG = 80, 81, 88
-    R_GS, R_GX, R_GA, R_GC = 96, 104, 105, 113
-    R_A, R_AC, R_S1, R_S2 = 114, 162, 171, 187
+    R_X, R_XO, R_W, R_PAIR, R_RING = 0, 8, 16, 24, 32
+    R_P, R_SHORT, R_LONG = 64, 65, 66
+    R_GS, R_GX, R_GA, R_GC = 67, 75, 76, 84
+    R_A, R_OWN, R_AC = 85, 133, 134
+    R_S1, R_S2, R_S3 = 150, 158, 159
 
     loads = [
         pltpu.make_async_copy(x_in, pk.at[0:32], lsem.at[0]),
@@ -95,7 +93,7 @@
         copy.start()
 
     barrier = pltpu.get_barrier_semaphore()
-    peers = [mdev(k) for k in range(1, NM)] + [across] + [pdev(k) for k in range(1, 16)]
+    peers = [mdev(k) for k in range(1, NM)] + [across, other] + [zdev(k) for k in range(1, NZ)]
     for peer in peers:
         pl.semaphore_signal(barrier, inc=1, device_id=peer, device_id_type=MESH)
 
@@ -134,12 +132,9 @@
         j = (m + NM - k) % NM
         got(xb.at[j], R_X + j)
         send(xb.at[j], xo.at[j], R_XO + j, other)
-    for k in range(NM):
-        j = (m + NM - k) % NM
-        got(xo.at[j], R_XO + j)
-
     place = lax.broadcasted_iota(jnp.int32, (128, W), 0) % 16
-    for src, dst in ((xb, va), (xo, vo)):
+
+    def spread(src, dst):
         rows = src[:, 64:80, :].reshape(128, W).astype(F32)
         for i in range(3):
             keep = jnp.logical_and(place >= 4 * i, place < 4 * i + 4)
@@ -148,64 +143,89 @@
     def tokens(ref, first):
         return ref[:, 32 * first : 32 * first + 32, :].reshape(TOK, W)
 
-    A, B = (0, 1, 2, 3), (4, 5, 6)
-    RIGHT, LEFT = 0, 1
-    to_dev = (right, left)
-
-    def first(way, slab, value):
-        ring_s[way, 0, slab] = value.astype(BF)
-        send(ring_s.at[way, 0, slab], ring_d.at[way, 0, slab], R_RING + way * 28 + slab, to_dev[way])
-
-    def arrived(way, s, slab):
-        got(ring_d.at[way, s - 1, slab], R_RING + (way * 4 + s - 1) * 7 + slab)
-
-    def onward(way, s, slab, step):
-        arrived(way, s, slab)
-        value = part[at(step), slab] + ring_d[way, s - 1, slab].astype(F32)
-        ring_s[way, s, slab] = value.astype(BF)
-        send(
-            ring_s.at[way, s, slab], ring_d.at[way, s, slab],
-            R_RING + (way * 4 + s) * 7 + slab, to_dev[way],
-        )
+    spread(xb, va)
+    val = jnp.zeros((NZ * HB, 128), F32)
+    for i in range(3):
+        lhs = wt[c, :, i].reshape(NZ * HB, W)
+        total = nt(lhs, tokens(xb, 1 if i == 2 else 0))
+        part[:, 0, i] = total[:, :128].reshape(NZ, HB, 128)
+        part[:, 1, i] = total[:, 128:].reshape(NZ, HB, 128)
+        val = val + nt(lhs, va[i])
+    vpart[...] = val.reshape(NZ, HB, 128)
+    for k in range(NM):
+        j = (m + NM - k) % NM
+        got(xo.at[j], R_XO + j)
+    spread(xo, vo)
+
+    def pair(step):
+        send(pair_s.at[at(step)], pair_d.at[at(step)], R_PAIR + at(step), across)
 
     far = at(4)
     got(wo.at[far], R_W + far)
+    away = xo[pl.ds(4 * (1 - xh), 4)]
     for i in range(3):
-        which = 1 if i == 2 else 0
-        total = nt(wt[c, far, i], tokens(xb, which)) + nt(wo[far, i], tokens(xo, which))
-        first(RIGHT, i, total[:, :128])
-        first(LEFT, 4 + i, total[:, 128:])
-    val = jnp.zeros((HB, 128), F32)
-    for i in range(3):
-        val = val + nt(wt[c, far, i], va[i]) + nt(wo[far, i], vo[i])
-    first(RIGHT, 3, val)
-
+        which = 32 if i == 2 else 0
+        total = nt(wo[far, i], away[:, which : which + 32, :].reshape(128, W))
+        pair_s[far, i] = (part[far, 1 - xh, i] + total).astype(BF)
+    pair(4)
     for k in range(1, NZ):
         got(wo.at[at(4 + k)], R_W + at(4 + k))
     val = jnp.zeros((NZ * HB, 128), F32)
     for i in range(3):
-        which = 1 if i == 2 else 0
-        lhs, lho = wt[c, :, i].reshape(NZ * HB, W), wo[:, i].reshape(NZ * HB, W)
-        total = nt(lhs, tokens(xb, which)) + nt(lho, tokens(xo, which))
-        part[:, i] = total[:, :128].reshape(NZ, HB, 128)
-        part[:, 4 + i] = total[:, 128:].reshape(NZ, HB, 128)
-        first(LEFT, i, part[at(-3), i])
-        first(RIGHT, 4 + i, part[at(3), 4 + i])
-        val = val + nt(lhs, va[i]) + nt(lho, vo[i])
-    part[:, 3] = val.reshape(NZ, HB, 128)
-    first(LEFT, 3, part[at(-3), 3])
-    send(part.at[z], swap_p, R_P, across)
+        lhs = wo[:, i].reshape(NZ * HB, W)
+        total = nt(lhs, tokens(xo, 1 if i == 2 else 0))
+        part[:, 0, i] = part[:, 0, i] + total[:, :128].reshape(NZ, HB, 128)
+        part[:, 1, i] = part[:, 1, i] + total[:, 128:].reshape(NZ, HB, 128)
+        val = val + nt(lhs, vo[i])
+    vpart[...] = vpart[...] + val.reshape(NZ, HB, 128)
+    for step in (3, -3, 2, -2, 1, -1, 0):
+        pair_s[at(step)] = part[at(step), 1 - xh].astype(BF)
+        pair(step)
+    send(vpart.at[z], swap_p, R_P, across)
+
+    A, B = (0, 1), (2, 3)
+    RIGHT, LEFT = 0, 1
+    to_dev = (right, left)
+
+    def here(step, slab):
+        if slab == 3:
+            return vpart[at(step)]
+        return part[at(step), xh, slab] + pair_d[at(step), slab].astype(F32)
+
+    def paired(step):
+        got(pair_d.at[at(step)], R_PAIR + at(step))
+
+    def wide(way, s, slab):
+        far_first = (slab in A) == (way == RIGHT)
+        return slab < 3 and s == (3 if far_first else 2)
+
+    def buffers(way, s, slab):
+        if wide(way, s, slab):
+            return last_s.at[way, slab], last_d.at[way, slab]
+        return ring_s.at[way, s, slab], ring_d.at[way, s, slab]
+
+    def ring(way, s, slab, value):
+        src, dst = buffers(way, s, slab)
+        src[...] = value.astype(src.dtype)
+        send(src, dst, R_RING + (way * 4 + s) * 4 + slab, to_dev[way])
+
+    def arrived(way, s, slab):
+        src, dst = buffers(way, s - 1, slab)
+        got(dst, R_RING + (way * 4 + s - 1) * 4 + slab)
+        return dst
+
+    def onward(way, s, slab, step):
+        dst = arrived(way, s, slab)
+        ring(way, s, slab, here(step, slab) + dst[...].astype(F32))
 
     def both_long(s):
-        for i in range(4):
+        for i in range(2):
             onward(RIGHT, s, A[i], 4 - s)
-            if i < 3:
-                onward(LEFT, s, B[i], s - 4)
+            onward(LEFT, s, B[i], s - 4)
 
     def both_short(s):
-        for i in range(4):
-            if i < 3:
-                onward(RIGHT, s, B[i], 3 - s)
+        for i in range(2):
+            onward(RIGHT, s, B[i], 3 - s)
             onward(LEFT, s, A[i], s - 3)
 
     def half(ref, which):
@@ -217,92 +237,112 @@
     for k in range(1, NZ):
         send(gram_s.at[at(k)], gram_d.at[z], R_GS + z, zdev(k))
 
+    paired(4)
+    for i in range(2):
+        ring(RIGHT, 0, A[i], here(4, A[i]))
+        ring(LEFT, 0, B[i], here(4, B[i]))
+    paired(3)
+    for i in range(2):
+        ring(RIGHT, 0, B[i], here(3, B[i]))
+    paired(-3)
+    for i in range(2):
+        ring(LEFT, 0, A[i], here(-3, A[i]))
     both_long(1)
-    both_short(1)
     for copy in loads[8:]:
         copy.wait()
     for k in range(1, NZ):
         got(gram_d.at[at(k)], R_GS + at(k))
     gram_x[0] = jnp.sum(gram_d[...], axis=0)
     send(gram_x.at[0], gram_x.at[1], R_GX, across)
+    paired(2)
+    paired(-2)
+    both_short(1)
     both_long(2)
-    both_short(2)
     got(gram_x.at[1], R_GX)
     gram_all[c, z] = gram_x[0] + gram_x[1]
     for k in range(1, NZ):
         send(gram_all.at[c, z], gram_all.at[c, z], R_GA + z, zdev(k))
+    paired(1)
+    paired(-1)
+    both_short(2)
     both_long(3)
 
-    def pass_on(way, s, slab, dst, rs):
-        arrived(way, s, slab)
-        send(ring_d.at[way, s - 1, slab], swap_d.at[dst, slab], rs + slab, across)
-
-    for i in range(4):
-        if i < 3:
-            pass_on(RIGHT, 3, B[i], 0, R_SHORT)
-        pass_on(LEFT, 3, A[i], 0, R_SHORT)
     r_row = jnp.zeros((1, TOK), F32)
     for e in range(EX):
         r_row = r_row + jnp.where(ids[...] == e, sw[e], 0.0)
     for i in range(2):
         xt[i] = tokens(xb, i).T.astype(F32)
+    paired(0)
     for k in range(1, NZ):
         got(gram_all.at[c, at(k)], R_GA + at(k))
     send(gram_all.at[c], gram_all.at[c], R_GC, other)
-    got(swap_p, R_P)
-    for i in range(4):
-        pass_on(RIGHT, 4, A[i], 1, R_LONG)
-        if i < 3:
-            pass_on(LEFT, 4, B[i], 1, R_LONG)
-
-    def whole(slab):
-        way = RIGHT if slab < 4 else LEFT
-        mine_ = part[z, slab] + ring_d[1 - way, 2, slab].astype(F32) + ring_d[way, 3, slab].astype(F32)
-        got(swap_d.at[0, slab], R_SHORT + slab)
-        got(swap_d.at[1, slab], R_LONG + slab)
-        theirs = swap_p[slab] + swap_d[0, slab].astype(F32) + swap_d[1, slab].astype(F32)
-        return mine_ + theirs
+    short_v = arrived(RIGHT, 3, 3)
+    send(short_v, swap_d.at[0], R_SHORT, across)
+
+    def ended(slab):
+        way = RIGHT if slab in A else LEFT
+        total = here(0, slab) + arrived(1 - way, 3, slab)[...].astype(F32)
+        return total + arrived(way, 4, slab)[...].astype(F32)
 
     def block_terms(gate, up, back):
         sig = 1.0 / (1.0 + jnp.exp(-gate))
         act = gate * sig
         return act * up, back * up * sig * (1.0 + gate * (1.0 - sig)), back * act
 
-    def gather(src, block, way, step, slab):
+    terms = block_terms(ended(0), ended(1), ended(2))
+
+    def gather(src, block, half, way, step, g, i):
         send(
-            src, full.at[block, slab], R_A + (way * 4 + step - 1) * 6 + slab, to_dev[way]
+            src, full.at[block, half, i],
+            R_A + ((way * 4 + step - 1) * 2 + g) * 3 + i, to_dev[way],
         )
 
-    for h in range(2):
-        terms = block_terms(*[whole(4 * h + i) for i in range(3)])
+    halves = (xh, 1 - xh)
+
+    def start_gather(g):
         for i in range(3):
-            own[3 * h + i] = terms[i].astype(BF)
-            gather(own.at[3 * h + i], slot, RIGHT, 1, 3 * h + i)
-            gather(own.at[3 * h + i], slot, LEFT, 1, 3 * h + i)
-    send(own, full.at[slot], R_AC + z, other)
+            for way in (RIGHT, LEFT):
+                gather(own.at[halves[g], i], slot, halves[g], way, 1, g, i)
+        send(own.at[halves[g]], full.at[slot, halves[g]], R_AC + 2 * z + g, other)
+
+    for i in range(3):
+        own[xh, i] = terms[i].astype(BF)
+    send(own.at[xh], own.at[xh], R_OWN, across)
+    start_gather(0)
+    long_v = arrived(LEFT, 4, 3)
+    send(long_v, swap_d.at[1], R_LONG, across)
+
+    def step_of_gather(step, g):
+        blocks = [2 * at(-step) + c, 2 * at(step) + c]
+        half = halves[g]
+        whole_way = [(0, 1), (2,)] if g == 0 else [(2,), (0, 1)]
+        for i in range(3):
+            for way in (RIGHT, LEFT):
+                if step == 4 and i not in whole_way[way]:
+                    continue
+                piece = full.at[blocks[way], half, i]
+                got(piece, R_A + ((way * 4 + step - 1) * 2 + g) * 3 + i)
+                if step < 3 or (step == 3 and i in whole_way[way]):
+                    gather(piece, blocks[way], half, way, step + 1, g, i)
+        for way, zz in ((RIGHT, at(-step)), (LEFT, at(step))):
+            if step < 4 or way == RIGHT:
+                send(full.at[blocks[way], half], full.at[blocks[way], half], R_AC + 2 * zz + g, other)
+
+    step_of_gather(1, 0)
+    got(own.at[1 - xh], R_OWN)
+    start_gather(1)
     outs = [pltpu.make_async_copy(own, full.at[slot], hsem.at[0])]
     outs[0].start()
-
-    def step_of_gather(step):
-        blocks = [2 * at(-step) + c, 2 * at(step) + c]
-        for i in range(6):
-            for way in (RIGHT, LEFT):
-                if step == 4 and i // 3 != way:
-                    continue
-                got(full.at[blocks[way], i], R_A + (way * 4 + step - 1) * 6 + i)
-                if step < 3 or (step == 3 and i // 3 == way):
-                    gather(full.at[blocks[way], i], blocks[way], way, step + 1, i)
-        if step < 4:
-            for way, zz in ((RIGHT, at(-step)), (LEFT, at(step))):
-                send(full.at[blocks[way]], full.at[blocks[way]], R_AC + zz, other)
-        else:
-            send(full.at[blocks[0]], full.at[blocks[0]], R_AC + at(4), other)
 
     got(gram_all.at[1 - c], R_GC)
     kt = jnp.concatenate([gram_all[0].reshape(128, 128), gram_all[1].reshape(128, 128)], axis=1)
     rk = (kt * r_row).astype(BF)
-    hb, dgb, dub = [jnp.concatenate([own[i], own[3 + i]], axis=1) for i in range(3)]
-    val = whole(3)
+    hb, dgb, dub = [jnp.concatenate([own[0, i], own[1, i]], axis=1) for i in range(3)]
+    got(swap_p, R_P)
+    got(swap_d.at[0], R_SHORT)
+    got(swap_d.at[1], R_LONG)
+    mine = vpart[z] + short_v[...].astype(F32) + long_v[...].astype(F32)
+    val = mine + (swap_p[...] + swap_d[0].astype(F32) + swap_d[1].astype(F32))
     v_gate = val - LEARN_RATE * nt(dgb, rk)
     v_up = pltpu.roll(val, 124, 1) - LEARN_RATE * nt(dub, rk)
     v_back = pltpu.roll(val - LEARN_RATE * nt(hb, rk), 120, 1)
@@ -319,24 +359,28 @@
     token = jnp.sum(inner * kt, axis=0, keepdims=True)
     label = lax.broadcasted_iota(jnp.int32, (EX, TOK), 0)
     score = jnp.sum(jnp.where(ids[...] == label, token, 0.0), axis=1, keepdims=True)
-    sc1[slot] = jnp.broadcast_to(score, (EX, 128))
-    for k in range(1, 16):
-        send(sc1.at[slot], sc1.at[slot], R_S1 + slot, pdev(k))
-
-    step_of_gather(1)
-    step_of_gather(2)
-    for k in range(1, 16):
-        j = (slot + k) % 16
-        got(sc1.at[j], R_S1 + j)
-    sc2[m] = jnp.sum(sc1[...], axis=0)
+    sc1[z] = jnp.broadcast_to(score, (EX, 128))
+    for k in range(1, NZ):
+        send(sc1.at[z], sc1.at[z], R_S1 + z, zdev(k))
+
+    step_of_gather(2, 0)
+    step_of_gather(1, 1)
+    step_of_gather(3, 0)
+    step_of_gather(2, 1)
+    for k in range(1, NZ):
+        got(sc1.at[at(k)], R_S1 + at(k))
+    sc2[c] = jnp.sum(sc1[...], axis=0)
+    send(sc2.at[c], sc2.at[c], R_S2, other)
+    step_of_gather(4, 0)
+    got(sc2.at[1 - c], R_S2)
+    sc3[m] = sc2[0] + sc2[1]
     for k in range(1, NM):
-        send(sc2.at[m], sc2.at[m], R_S2 + m, mdev(k))
-
-    step_of_gather(3)
+        send(sc3.at[m], sc3.at[m], R_S3 + m, mdev(k))
+    step_of_gather(3, 1)
     for k in range(1, NM):
         j = (m + k) % NM
-        got(sc2.at[j], R_S2 + j)
-    score = jnp.sum(sc2[...], axis=0)
+        got(sc3.at[j], R_S3 + j)
+    score = jnp.sum(sc3[...], axis=0)
     rms = jnp.sqrt(jnp.mean(score * score, axis=0, keepdims=True) + 1e-6)
     arg = score / (4.0 * rms)
     soft = jnp.maximum(arg, 0.0) + jnp.log(1.0 + jnp.exp(-jnp.abs(arg)))
@@ -352,9 +396,10 @@
     copy.start()
     outs.append(copy)
 
-    step_of_gather(4)
-    for k in range(NZ):
-        got(full.at[2 * at(k) + 1 - c], R_AC + at(k))
+    step_of_gather(4, 1)
+    for g in range(2):
+        for k in range(NZ):
+            got(full.at[2 * at(k) + 1 - c, halves[g]], R_AC + 2 * at(k) + g)
     for copy in sends:
         copy.wait_send()
     for copy in outs:
@@ -364,7 +409,7 @@
 def grad_kernel(full, xs, wts, gg, gu, gd, out):
     def rows(i):
         return jnp.concatenate(
-            [full[:, i].reshape(8 * HB, 128), full[:, 3 + i].reshape(8 * HB, 128)], axis=1
+            [full[:, 0, i].reshape(8 * HB, 128), full[:, 1, i].reshape(8 * HB, 128)], axis=1
         )
 
     out[...] = wts[...]
@@ -381,7 +426,7 @@
     full, xs, wts = pl.pallas_call(
         comm_kernel,
         out_shape=(
-            jax.ShapeDtypeStruct((16, 6, HB, 128), BF),
+            jax.ShapeDtypeStruct((16, 2, 3, HB, 128), BF),
             jax.ShapeDtypeStruct((2, W, TOK), BF),
             jax.ShapeDtypeStruct((1, EX), F32),
         ),
@@ -401,17 +446,23 @@
             V((NM, 80, W), BF),
             V((3, 128, W), BF),
             V((3, 128, W), BF),
-            V((NZ, 7, HB, 128), F32),
-            V((6, HB, 128), BF),
-            V((2, 4, 7, HB, 128), BF),
-            V((2, 4, 7, HB, 128), BF),
-            V((7, HB, 128), F32),
-            V((2, 7, HB, 128), BF),
+            V((NZ, 2, 3, HB, 128), F32),
+            V((NZ, HB, 128), F32),
+            V((2, 3, HB, 128), BF),
+            V((NZ, 3, HB, 128), BF),
+            V((NZ, 3, HB, 128), BF),
+            V((2, 4, 4, HB, 128), BF),
+            V((2, 4, 4, HB, 128), BF),
+            V((2, 3, HB, 128), F32),
+            V((2, 3, HB, 128), F32),
+            V((HB, 128), F32),
+            V((2, HB, 128), BF),
             V((NZ, 16, 128), F32),
             V((NZ, 16, 128), F32),
             V((2, 16, 128), F32),
             V((2, NZ, 16, 128), F32),
-            V((16, EX, 128), F32),
+            V((NZ, EX, 128), F32),
+            V((2, EX, 128), F32),
             V((NM, EX, 128), F32),
             V((2, W, TOK), F32),
             V((2, W, TOK), BF),
@@ -443,7 +494,7 @@
             jax.ShapeDtypeStruct((1, EX), F32),
         ),
         in_specs=[
-            pl.BlockSpec((8, 6, HB, 128), lambda i: (i, 0, 0, 0)),
+            pl.BlockSpec((8, 2, 3, HB, 128), lambda i: (i, 0, 0, 0, 0)),
             pl.BlockSpec((2, W, TOK), lambda i: (0, 0, 0)),
             pl.BlockSpec((1, EX), lambda i: (0, 0)),
         ],

time: 70 us -> 73.1 us (1.044)
  Pallas kernels: 69.3 us -> 72.4 us
    pallas_call x1, Pallas kernels: 67.1 us -> 70.2 us  [body(): pl.pallas_call(comm_kernel, out_shape=(jax.ShapeDtypeStruct((16, 2, 3, HB...]
where the time goes in v3:
time: 73.1 us; the launch traced here: 73 us
  Pallas kernels  72.4 us (99%)
    pallas_call x1, Pallas kernels, body(): pl.pallas_call(comm_kernel, out_shape=(jax.ShapeDtypeStruct((16, 2, 3, HB...  70.2 us
    pallas_call x1, Pallas kernels, body(): pl.pallas_call(grad_kernel, grid=(2,), out_shape=(jax.ShapeDtypeStruct((W...  2.18 us

profile of v3, /device:TPU:1, one launch (start us, length us, event | category | flops | bytes accessed | tf_op | source)
XLA Modules:
  0.0 73.0 jit_solution(10884442006878783276)
XLA Ops:
  0.6 70.2 %reduce_and_gather.1 = (bf16[16,2,3,112,128]{4,3,2,1,0:T(8,128)(2,1)S(1)}, bf16[2,256,256]{2,1,0:T(8,128)(2,1)S(1)}, f32[1,8]{1,0:T(1,128)S(1)}) custom-call(bf16[32,256]{1,0:T(8,128)(2,1)} %x_in.1, bf16[32,256]{1,0:T(8,128)(2,1)} %c_in.1, bf16[4,256]{1,0:T(4,128)(2,1)} %vx_in.1, bf16[4,256]{1,0:T(4,128)(2,1)} %vc_in.1, bf16[256,1792]{1,0:T(8,128)(2,1)} %wg_in.1, ...), custom_call_target="tpu_custom_call" | custom-call | tf_op jit(solution)/shard_map/reduce_and_gather/pallas_call | solution.py:426
  70.8 2.2 %gradients.1 = (bf16[256,1792]{1,0:T(8,128)(2,1)}, bf16[256,1792]{1,0:T(8,128)(2,1)}, bf16[1792,256]{1,0:T(8,128)(2,1)}, f32[1,8]{1,0:T(1,128)}) custom-call(bf16[16,2,3,112,128]{4,3,2,1,0:T(8,128)(2,1)S(1)} %get-tuple-element.11.full, bf16[2,256,256]{2,1,0:T(8,128)(2,1)S(1)} %get-tuple-element.12.xs, f32[1,8]{1,0:T(1,128)S(1)} %get-tuple-element.13.wts), custom_call_target="tpu_custom_call" | custom-call | tf_op jit(solution)/shard_map/gradients/pallas_call | solution.py:487

commit v4 on v2

--- a/solution.py
+++ b/solution.py
@@ -30,7 +30,7 @@
     x_in, c_in, vx_in, vc_in, wg_in, wu_in, wd_in, sw_in, ids_in, mask_in,
     full, xs_out, wts_out,
     sw, ids, mask, vraw, wraw, wt, wo, pk, vstage, xb, xo, va, vo, part, own,
-    ring_s, ring_d, swap_p, swap_d, gram_s, gram_d, gram_x, gram_all, sc1, sc2, xt, xs,
+    ring_s, ring_d, swap_p, swap_d, gram_s, gram_d, gram_x, gram_all, sc1, sc2, sc3, xt, xs,
     lsem, ssem, rsem, hsem,
 ):
     d = lax.axis_index("dp")
@@ -52,15 +52,17 @@
     def mdev(step):
         return (d, (m + step) % NM)
 
-    def pdev(step):
-        j = (slot + step) % 16
-        return dev(j // 2, xh, j % 2)
-
     other = dev(z, xh, 1 - c)
     across = dev(z, 1 - xh, c)
     right, left = zdev(1), zdev(-1)
 
     sends = []
+    ended = [0]
+
+    def drain(to):
+        for copy in sends[ended[0] : to]:
+            copy.wait_send()
+        ended[0] = to
 
     def send(src, dst, rs, to):
         copy = pltpu.make_async_remote_copy(
@@ -76,7 +78,7 @@
     R_X, R_XO, R_W, R_RING = 0, 8, 16, 24
     R_P, R_SHORT, R_LONG = 80, 81, 88
     R_GS, R_GX, R_GA, R_GC = 96, 104, 105, 113
-    R_A, R_AC, R_S1, R_S2 = 114, 162, 171, 187
+    R_A, R_AC, R_S1, R_S2, R_S3 = 114, 162, 171, 179, 180
 
     loads = [
         pltpu.make_async_copy(x_in, pk.at[0:32], lsem.at[0]),
@@ -95,7 +97,7 @@
         copy.start()
 
     barrier = pltpu.get_barrier_semaphore()
-    peers = [mdev(k) for k in range(1, NM)] + [across] + [pdev(k) for k in range(1, 16)]
+    peers = [mdev(k) for k in range(1, NM)] + [across, other] + [zdev(k) for k in range(1, NZ)]
     for peer in peers:
         pl.semaphore_signal(barrier, inc=1, device_id=peer, device_id_type=MESH)
 
@@ -134,12 +136,9 @@
         j = (m + NM - k) % NM
         got(xb.at[j], R_X + j)
         send(xb.at[j], xo.at[j], R_XO + j, other)
-    for k in range(NM):
-        j = (m + NM - k) % NM
-        got(xo.at[j], R_XO + j)
-
     place = lax.broadcasted_iota(jnp.int32, (128, W), 0) % 16
-    for src, dst in ((xb, va), (xo, vo)):
+
+    def spread(src, dst):
         rows = src[:, 64:80, :].reshape(128, W).astype(F32)
         for i in range(3):
             keep = jnp.logical_and(place >= 4 * i, place < 4 * i + 4)
@@ -147,6 +146,19 @@
 
     def tokens(ref, first):
         return ref[:, 32 * first : 32 * first + 32, :].reshape(TOK, W)
+
+    spread(xb, va)
+    val = jnp.zeros((NZ * HB, 128), F32)
+    for i in range(3):
+        lhs = wt[c, :, i].reshape(NZ * HB, W)
+        total = nt(lhs, tokens(xb, 1 if i == 2 else 0))
+        part[:, i] = total[:, :128].reshape(NZ, HB, 128)
+        part[:, 4 + i] = total[:, 128:].reshape(NZ, HB, 128)
+        val = val + nt(lhs, va[i])
+    part[:, 3] = val.reshape(NZ, HB, 128)
+    for k in range(NM):
+        j = (m + NM - k) % NM
+        got(xo.at[j], R_XO + j)
 
     A, B = (0, 1, 2, 3), (4, 5, 6)
     RIGHT, LEFT = 0, 1
@@ -171,28 +183,27 @@
     far = at(4)
     got(wo.at[far], R_W + far)
     for i in range(3):
-        which = 1 if i == 2 else 0
-        total = nt(wt[c, far, i], tokens(xb, which)) + nt(wo[far, i], tokens(xo, which))
-        first(RIGHT, i, total[:, :128])
-        first(LEFT, 4 + i, total[:, 128:])
-    val = jnp.zeros((HB, 128), F32)
+        total = nt(wo[far, i], tokens(xo, 1 if i == 2 else 0))
+        first(RIGHT, i, part[far, i] + total[:, :128])
+        first(LEFT, 4 + i, part[far, 4 + i] + total[:, 128:])
+    spread(xo, vo)
+    val = part[far, 3]
     for i in range(3):
-        val = val + nt(wt[c, far, i], va[i]) + nt(wo[far, i], vo[i])
+        val = val + nt(wo[far, i], vo[i])
     first(RIGHT, 3, val)
 
     for k in range(1, NZ):
         got(wo.at[at(4 + k)], R_W + at(4 + k))
     val = jnp.zeros((NZ * HB, 128), F32)
     for i in range(3):
-        which = 1 if i == 2 else 0
-        lhs, lho = wt[c, :, i].reshape(NZ * HB, W), wo[:, i].reshape(NZ * HB, W)
-        total = nt(lhs, tokens(xb, which)) + nt(lho, tokens(xo, which))
-        part[:, i] = total[:, :128].reshape(NZ, HB, 128)
-        part[:, 4 + i] = total[:, 128:].reshape(NZ, HB, 128)
+        lhs = wo[:, i].reshape(NZ * HB, W)
+        total = nt(lhs, tokens(xo, 1 if i == 2 else 0))
+        part[:, i] = part[:, i] + total[:, :128].reshape(NZ, HB, 128)
+        part[:, 4 + i] = part[:, 4 + i] + total[:, 128:].reshape(NZ, HB, 128)
         first(LEFT, i, part[at(-3), i])
         first(RIGHT, 4 + i, part[at(3), 4 + i])
-        val = val + nt(lhs, va[i]) + nt(lho, vo[i])
-    part[:, 3] = val.reshape(NZ, HB, 128)
+        val = val + nt(lhs, vo[i])
+    part[:, 3] = part[:, 3] + val.reshape(NZ, HB, 128)
     first(LEFT, 3, part[at(-3), 3])
     send(part.at[z], swap_p, R_P, across)
 
@@ -217,6 +228,7 @@
     for k in range(1, NZ):
         send(gram_s.at[at(k)], gram_d.at[z], R_GS + z, zdev(k))
 
+    drain(len(sends) - 40)
     both_long(1)
     both_short(1)
     for copy in loads[8:]:
@@ -232,6 +244,7 @@
     for k in range(1, NZ):
         send(gram_all.at[c, z], gram_all.at[c, z], R_GA + z, zdev(k))
     both_long(3)
+    older = len(sends) - 7
 
     def pass_on(way, s, slab, dst, rs):
         arrived(way, s, slab)
@@ -319,24 +332,29 @@
     token = jnp.sum(inner * kt, axis=0, keepdims=True)
     label = lax.broadcasted_iota(jnp.int32, (EX, TOK), 0)
     score = jnp.sum(jnp.where(ids[...] == label, token, 0.0), axis=1, keepdims=True)
-    sc1[slot] = jnp.broadcast_to(score, (EX, 128))
-    for k in range(1, 16):
-        send(sc1.at[slot], sc1.at[slot], R_S1 + slot, pdev(k))
+    sc1[z] = jnp.broadcast_to(score, (EX, 128))
+    for k in range(1, NZ):
+        send(sc1.at[z], sc1.at[z], R_S1 + z, zdev(k))
 
     step_of_gather(1)
+    drain(older)
     step_of_gather(2)
-    for k in range(1, 16):
-        j = (slot + k) % 16
-        got(sc1.at[j], R_S1 + j)
-    sc2[m] = jnp.sum(sc1[...], axis=0)
+    for k in range(1, NZ):
+        got(sc1.at[at(k)], R_S1 + at(k))
+    sc2[c] = jnp.sum(sc1[...], axis=0)
+    send(sc2.at[c], sc2.at[c], R_S2, other)
+    got(sc2.at[1 - c], R_S2)
+    sc3[m] = sc2[0] + sc2[1]
     for k in range(1, NM):
-        send(sc2.at[m], sc2.at[m], R_S2 + m, mdev(k))
+        send(sc3.at[m], sc3.at[m], R_S3 + m, mdev(k))
+    older = len(sends) - 45
 
     step_of_gather(3)
+    drain(older)
     for k in range(1, NM):
         j = (m + k) % NM
-        got(sc2.at[j], R_S2 + j)
-    score = jnp.sum(sc2[...], axis=0)
+        got(sc3.at[j], R_S3 + j)
+    score = jnp.sum(sc3[...], axis=0)
     rms = jnp.sqrt(jnp.mean(score * score, axis=0, keepdims=True) + 1e-6)
     arg = score / (4.0 * rms)
     soft = jnp.maximum(arg, 0.0) + jnp.log(1.0 + jnp.exp(-jnp.abs(arg)))
@@ -355,8 +373,7 @@
     step_of_gather(4)
     for k in range(NZ):
         got(full.at[2 * at(k) + 1 - c], R_AC + at(k))
-    for copy in sends:
-        copy.wait_send()
+    drain(len(sends))
     for copy in outs:
         copy.wait()
 
@@ -411,7 +428,8 @@
             V((NZ, 16, 128), F32),
             V((2, 16, 128), F32),
             V((2, NZ, 16, 128), F32),
-            V((16, EX, 128), F32),
+            V((NZ, EX, 128), F32),
+            V((2, EX, 128), F32),
             V((NM, EX, 128), F32),
             V((2, W, TOK), F32),
             V((2, W, TOK), BF),

time: 70 us -> 68.1 us (0.973)
  Pallas kernels: 69.3 us -> 67.4 us
    pallas_call x1, Pallas kernels: 67.1 us -> 65.2 us  [body(): pl.pallas_call(comm_kernel, out_shape=(jax.ShapeDtypeStruct((16, 6, HB, 1...]
where the time goes in v4:
time: 68.1 us; the launch traced here: 68 us
  Pallas kernels  67.4 us (99%)
    pallas_call x1, Pallas kernels, body(): pl.pallas_call(comm_kernel, out_shape=(jax.ShapeDtypeStruct((16, 6, HB, 1...  65.2 us
    pallas_call x1, Pallas kernels, body(): pl.pallas_call(grad_kernel, grid=(2,), out_shape=(jax.ShapeDtypeStruct((W...  2.18 us

profile of v4, /device:TPU:1, one launch (start us, length us, event | category | flops | bytes accessed | tf_op | source)
XLA Modules:
  0.0 68.0 jit_solution(9118591297071645053)
XLA Ops:
  0.6 65.2 %reduce_and_gather.1 = (bf16[16,6,112,128]{3,2,1,0:T(8,128)(2,1)S(1)}, bf16[2,256,256]{2,1,0:T(8,128)(2,1)S(1)}, f32[1,8]{1,0:T(1,128)S(1)}) custom-call(bf16[32,256]{1,0:T(8,128)(2,1)} %x_in.1, bf16[32,256]{1,0:T(8,128)(2,1)} %c_in.1, bf16[4,256]{1,0:T(4,128)(2,1)} %vx_in.1, bf16[4,256]{1,0:T(4,128)(2,1)} %vc_in.1, bf16[256,1792]{1,0:T(8,128)(2,1)} %wg_in.1, ...), custom_call_target="tpu_custom_call" | custom-call | tf_op jit(solution)/shard_map/reduce_and_gather/pallas_call | solution.py:398
  65.8 2.2 %gradients.1 = (bf16[256,1792]{1,0:T(8,128)(2,1)}, bf16[256,1792]{1,0:T(8,128)(2,1)}, bf16[1792,256]{1,0:T(8,128)(2,1)}, f32[1,8]{1,0:T(1,128)}) custom-call(bf16[16,6,112,128]{3,2,1,0:T(8,128)(2,1)S(1)} %get-tuple-element.11.full, bf16[2,256,256]{2,1,0:T(8,128)(2,1)S(1)} %get-tuple-element.12.xs, f32[1,8]{1,0:T(1,128)S(1)} %get-tuple-element.13.wts), custom_call_target="tpu_custom_call" | custom-call | tf_op jit(solution)/shard_map/gradients/pallas_call | solution.py:454

commit v5 on v4

--- a/solution.py
+++ b/solution.py
@@ -56,29 +56,19 @@
     across = dev(z, 1 - xh, c)
     right, left = zdev(1), zdev(-1)
 
-    sends = []
-    ended = [0]
-
-    def drain(to):
-        for copy in sends[ended[0] : to]:
-            copy.wait_send()
-        ended[0] = to
-
-    def send(src, dst, rs, to):
-        copy = pltpu.make_async_remote_copy(
-            src_ref=src, dst_ref=dst, send_sem=ssem.at[len(sends)], recv_sem=rsem.at[rs],
+    def send(src, dst, ss, rs, to):
+        pltpu.make_async_remote_copy(
+            src_ref=src, dst_ref=dst, send_sem=ssem.at[ss], recv_sem=rsem.at[rs],
             device_id=to, device_id_type=MESH,
-        )
-        copy.start()
-        sends.append(copy)
+        ).start()
 
     def got(dst, rs):
         pltpu.make_async_copy(dst, dst, rsem.at[rs]).wait()
 
-    R_X, R_XO, R_W, R_RING = 0, 8, 16, 24
-    R_P, R_SHORT, R_LONG = 80, 81, 88
-    R_GS, R_GX, R_GA, R_GC = 96, 104, 105, 113
-    R_A, R_AC, R_S1, R_S2, R_S3 = 114, 162, 171, 179, 180
+    R_X, R_XO, R_W, R_P, R_GS, R_GX, R_GA, R_GC, R_AC, R_S1, R_S2, R_S3 = 0, 8, 9, 11, 12, 13, 14, 15, 16, 17, 18, 19
+    R_SHORT, R_LONG, R_RING, R_A = 20, 27, 34, 83
+
+    (S_X, S_W, S_XO, S_RING, S_LAST, S_P, S_SHORT, S_LONG, S_GS, S_GX, S_GA, S_GC, S_A, S_AC, S_S1, S_S2, S_S3) = range(17)
 
     loads = [
         pltpu.make_async_copy(x_in, pk.at[0:32], lsem.at[0]),
@@ -114,8 +104,8 @@
     pl.semaphore_wait(barrier, len(peers))
 
     for k in range(1, NM):
-        send(pk, xb.at[m], R_X + m, mdev(k))
-    send(pk, xo.at[m], R_XO + m, other)
+        send(pk, xb.at[m], S_X, R_X + m, mdev(k))
+    send(pk, xo.at[m], S_X, R_XO, other)
 
     for w in range(2):
         loads[2 + w].wait()
@@ -130,12 +120,12 @@
     loads[6].wait()
     loads[7].wait()
     for step in (4, 3, 5, 2, 6, 1, 7, 0):
-        send(wt.at[1 - c, at(step)], wo.at[at(step)], R_W + at(step), other)
+        send(wt.at[1 - c, at(step)], wo.at[at(step)], S_W, R_W if step == 4 else R_W + 1, other)
 
     for k in range(1, NM):
         j = (m + NM - k) % NM
         got(xb.at[j], R_X + j)
-        send(xb.at[j], xo.at[j], R_XO + j, other)
+        send(xb.at[j], xo.at[j], S_XO, R_XO, other)
     place = lax.broadcasted_iota(jnp.int32, (128, W), 0) % 16
 
     def spread(src, dst):
@@ -156,32 +146,36 @@
         part[:, 4 + i] = total[:, 128:].reshape(NZ, HB, 128)
         val = val + nt(lhs, va[i])
     part[:, 3] = val.reshape(NZ, HB, 128)
-    for k in range(NM):
-        j = (m + NM - k) % NM
-        got(xo.at[j], R_XO + j)
+    got(xo, R_XO)
 
     A, B = (0, 1, 2, 3), (4, 5, 6)
     RIGHT, LEFT = 0, 1
     to_dev = (right, left)
 
-    def first(way, slab, value):
-        ring_s[way, 0, slab] = value.astype(BF)
-        send(ring_s.at[way, 0, slab], ring_d.at[way, 0, slab], R_RING + way * 28 + slab, to_dev[way])
-
-    def arrived(way, s, slab):
-        got(ring_d.at[way, s - 1, slab], R_RING + (way * 4 + s - 1) * 7 + slab)
-
-    def onward(way, s, slab, step):
-        arrived(way, s, slab)
-        value = part[at(step), slab] + ring_d[way, s - 1, slab].astype(F32)
+    def ring_sem(way, s, slab):
+        if s < 3:
+            return R_RING + (way * 3 + s) * 7 + slab
+        return R_RING + 42 + slab
+
+    def ring(way, s, slab, value):
         ring_s[way, s, slab] = value.astype(BF)
         send(
             ring_s.at[way, s, slab], ring_d.at[way, s, slab],
-            R_RING + (way * 4 + s) * 7 + slab, to_dev[way],
+            S_LAST if s == 3 else S_RING, ring_sem(way, s, slab), to_dev[way],
         )
 
+    def first(way, slab, value):
+        ring(way, 0, slab, value)
+
+    def arrived(way, s, slab):
+        got(ring_d.at[way, s - 1, slab], ring_sem(way, s - 1, slab))
+
+    def onward(way, s, slab, step):
+        arrived(way, s, slab)
+        ring(way, s, slab, part[at(step), slab] + ring_d[way, s - 1, slab].astype(F32))
+
     far = at(4)
-    got(wo.at[far], R_W + far)
+    got(wo.at[far], R_W)
     for i in range(3):
         total = nt(wo[far, i], tokens(xo, 1 if i == 2 else 0))
         first(RIGHT, i, part[far, i] + total[:, :128])
@@ -192,8 +186,7 @@
         val = val + nt(wo[far, i], vo[i])
     first(RIGHT, 3, val)
 
-    for k in range(1, NZ):
-        got(wo.at[at(4 + k)], R_W + at(4 + k))
+    got(wo.at[0:7], R_W + 1)
     val = jnp.zeros((NZ * HB, 128), F32)
     for i in range(3):
         lhs = wo[:, i].reshape(NZ * HB, W)
@@ -205,7 +198,7 @@
         val = val + nt(lhs, vo[i])
     part[:, 3] = part[:, 3] + val.reshape(NZ, HB, 128)
     first(LEFT, 3, part[at(-3), 3])
-    send(part.at[z], swap_p, R_P, across)
+    send(part.at[z], swap_p, S_P, R_P, across)
 
     def both_long(s):
         for i in range(4):
@@ -226,47 +219,43 @@
     gram_s[...] = gram.reshape(NZ, 16, 128)
     gram_d[z] = gram_s[z]
     for k in range(1, NZ):
-        send(gram_s.at[at(k)], gram_d.at[z], R_GS + z, zdev(k))
-
-    drain(len(sends) - 40)
+        send(gram_s.at[at(k)], gram_d.at[z], S_GS, R_GS, zdev(k))
+
     both_long(1)
     both_short(1)
     for copy in loads[8:]:
         copy.wait()
-    for k in range(1, NZ):
-        got(gram_d.at[at(k)], R_GS + at(k))
+    got(gram_d.at[0:7], R_GS)
     gram_x[0] = jnp.sum(gram_d[...], axis=0)
-    send(gram_x.at[0], gram_x.at[1], R_GX, across)
+    send(gram_x.at[0], gram_x.at[1], S_GX, R_GX, across)
     both_long(2)
     both_short(2)
     got(gram_x.at[1], R_GX)
     gram_all[c, z] = gram_x[0] + gram_x[1]
     for k in range(1, NZ):
-        send(gram_all.at[c, z], gram_all.at[c, z], R_GA + z, zdev(k))
+        send(gram_all.at[c, z], gram_all.at[c, z], S_GA, R_GA, zdev(k))
     both_long(3)
-    older = len(sends) - 7
-
-    def pass_on(way, s, slab, dst, rs):
+
+    def pass_on(way, s, slab, dst, ss, rs):
         arrived(way, s, slab)
-        send(ring_d.at[way, s - 1, slab], swap_d.at[dst, slab], rs + slab, across)
+        send(ring_d.at[way, s - 1, slab], swap_d.at[dst, slab], ss, rs + slab, across)
 
     for i in range(4):
         if i < 3:
-            pass_on(RIGHT, 3, B[i], 0, R_SHORT)
-        pass_on(LEFT, 3, A[i], 0, R_SHORT)
+            pass_on(RIGHT, 3, B[i], 0, S_SHORT, R_SHORT)
+        pass_on(LEFT, 3, A[i], 0, S_SHORT, R_SHORT)
     r_row = jnp.zeros((1, TOK), F32)
     for e in range(EX):
         r_row = r_row + jnp.where(ids[...] == e, sw[e], 0.0)
     for i in range(2):
         xt[i] = tokens(xb, i).T.astype(F32)
-    for k in range(1, NZ):
-        got(gram_all.at[c, at(k)], R_GA + at(k))
-    send(gram_all.at[c], gram_all.at[c], R_GC, other)
+    got(gram_all.at[c, 0:7], R_GA)
+    send(gram_all.at[c], gram_all.at[c], S_GC, R_GC, other)
     got(swap_p, R_P)
     for i in range(4):
-        pass_on(RIGHT, 4, A[i], 1, R_LONG)
+        pass_on(RIGHT, 4, A[i], 1, S_LONG, R_LONG)
         if i < 3:
-            pass_on(LEFT, 4, B[i], 1, R_LONG)
+            pass_on(LEFT, 4, B[i], 1, S_LONG, R_LONG)
 
     def whole(slab):
         way = RIGHT if slab < 4 else LEFT
@@ -281,10 +270,13 @@
         act = gate * sig
         return act * up, back * up * sig * (1.0 + gate * (1.0 - sig)), back * act
 
+    def gather_sem(way, step, slab):
+        if step < 4:
+            return R_A + (way * 3 + step - 1) * 6 + slab
+        return R_A + 36 + slab
+
     def gather(src, block, way, step, slab):
-        send(
-            src, full.at[block, slab], R_A + (way * 4 + step - 1) * 6 + slab, to_dev[way]
-        )
+        send(src, full.at[block, slab], S_A, gather_sem(way, step, slab), to_dev[way])
 
     for h in range(2):
         terms = block_terms(*[whole(4 * h + i) for i in range(3)])
@@ -292,7 +284,7 @@
             own[3 * h + i] = terms[i].astype(BF)
             gather(own.at[3 * h + i], slot, RIGHT, 1, 3 * h + i)
             gather(own.at[3 * h + i], slot, LEFT, 1, 3 * h + i)
-    send(own, full.at[slot], R_AC + z, other)
+    send(own, full.at[slot], S_AC, R_AC, other)
     outs = [pltpu.make_async_copy(own, full.at[slot], hsem.at[0])]
     outs[0].start()
 
@@ -302,14 +294,14 @@
             for way in (RIGHT, LEFT):
                 if step == 4 and i // 3 != way:
                     continue
-                got(full.at[blocks[way], i], R_A + (way * 4 + step - 1) * 6 + i)
+                got(full.at[blocks[way], i], gather_sem(way, step, i))
                 if step < 3 or (step == 3 and i // 3 == way):
                     gather(full.at[blocks[way], i], blocks[way], way, step + 1, i)
         if step < 4:
-            for way, zz in ((RIGHT, at(-step)), (LEFT, at(step))):
-                send(full.at[blocks[way]], full.at[blocks[way]], R_AC + zz, other)
+            for way in (RIGHT, LEFT):
+                send(full.at[blocks[way]], full.at[blocks[way]], S_AC, R_AC, other)
         else:
-            send(full.at[blocks[0]], full.at[blocks[0]], R_AC + at(4), other)
+            send(full.at[blocks[0]], full.at[blocks[0]], S_AC, R_AC, other)
 
     got(gram_all.at[1 - c], R_GC)
     kt = jnp.concatenate([gram_all[0].reshape(128, 128), gram_all[1].reshape(128, 128)], axis=1)
@@ -334,26 +326,20 @@
     score = jnp.sum(jnp.where(ids[...] == label, token, 0.0), axis=1, keepdims=True)
     sc1[z] = jnp.broadcast_to(score, (EX, 128))
     for k in range(1, NZ):
-        send(sc1.at[z], sc1.at[z], R_S1 + z, zdev(k))
+        send(sc1.at[z], sc1.at[z], S_S1, R_S1, zdev(k))
 
     step_of_gather(1)
-    drain(older)
     step_of_gather(2)
-    for k in range(1, NZ):
-        got(sc1.at[at(k)], R_S1 + at(k))
+    got(sc1.at[0:7], R_S1)
     sc2[c] = jnp.sum(sc1[...], axis=0)
-    send(sc2.at[c], sc2.at[c], R_S2, other)
+    send(sc2.at[c], sc2.at[c], S_S2, R_S2, other)
     got(sc2.at[1 - c], R_S2)
     sc3[m] = sc2[0] + sc2[1]
     for k in range(1, NM):
-        send(sc3.at[m], sc3.at[m], R_S3 + m, mdev(k))
-    older = len(sends) - 45
+        send(sc3.at[m], sc3.at[m], S_S3, R_S3, mdev(k))
 
     step_of_gather(3)
-    drain(older)
-    for k in range(1, NM):
-        j = (m + k) % NM
-        got(sc3.at[j], R_S3 + j)
+    got(sc3.at[0:7], R_S3)
     score = jnp.sum(sc3[...], axis=0)
     rms = jnp.sqrt(jnp.mean(score * score, axis=0, keepdims=True) + 1e-6)
     arg = score / (4.0 * rms)
@@ -371,9 +357,14 @@
     outs.append(copy)
 
     step_of_gather(4)
-    for k in range(NZ):
-        got(full.at[2 * at(k) + 1 - c], R_AC + at(k))
-    drain(len(sends))
+    got(full.at[0:8], R_AC)
+    for ref, ss in (
+        (xb, S_X), (wo, S_W), (xb.at[0:7], S_XO), (ring_s.at[:, 0:3], S_RING), (swap_d.at[0], S_LAST), (swap_p, S_P),
+        (swap_d.at[0], S_SHORT), (swap_d.at[1], S_LONG), (gram_d.at[0:7], S_GS), (gram_x.at[0], S_GX),
+        (gram_all.at[0, 0:7], S_GA), (gram_all.at[0], S_GC), (full.at[0:7], S_A), (full.at[0:8], S_AC),
+        (sc1.at[0:7], S_S1), (sc2.at[0], S_S2), (sc3.at[0:7], S_S3),
+    ):
+        pltpu.make_async_copy(ref, ref, ssem.at[ss]).wait()
     for copy in outs:
         copy.wait()
 
@@ -434,8 +425,8 @@
             V((2, W, TOK), F32),
             V((2, W, TOK), BF),
             pltpu.SemaphoreType.DMA((11,)),
-            pltpu.SemaphoreType.DMA((200,)),
-            pltpu.SemaphoreType.DMA((195,)),
+            pltpu.SemaphoreType.DMA((17,)),
+            pltpu.SemaphoreType.DMA((125,)),
             pltpu.SemaphoreType.DMA((2,)),
         ],
         compiler_params=pltpu.CompilerParams(

time: 68.1 us -> 65.8 us (0.966)
  Pallas kernels: 67.4 us -> 65.1 us
    pallas_call x1, Pallas kernels: 65.2 us -> 62.9 us  [body(): pl.pallas_call(comm_kernel, out_shape=(jax.ShapeDtypeStruct((16, 6, HB, 1...]
where the time goes in v5:
time: 65.8 us; the launch traced here: 65.7 us
  Pallas kernels  65.1 us (99%)
    pallas_call x1, Pallas kernels, body(): pl.pallas_call(comm_kernel, out_shape=(jax.ShapeDtypeStruct((16, 6, HB, 1...  62.9 us
    pallas_call x1, Pallas kernels, body(): pl.pallas_call(grad_kernel, grid=(2,), out_shape=(jax.ShapeDtypeStruct((W...  2.18 us

profile of v5, /device:TPU:1, one launch (start us, length us, event | category | flops | bytes accessed | tf_op | source)
XLA Modules:
  0.0 65.7 jit_solution(3045888749055369307)
XLA Ops:
  0.6 62.9 %reduce_and_gather.1 = (bf16[16,6,112,128]{3,2,1,0:T(8,128)(2,1)S(1)}, bf16[2,256,256]{2,1,0:T(8,128)(2,1)S(1)}, f32[1,8]{1,0:T(1,128)S(1)}) custom-call(bf16[32,256]{1,0:T(8,128)(2,1)} %x_in.1, bf16[32,256]{1,0:T(8,128)(2,1)} %c_in.1, bf16[4,256]{1,0:T(4,128)(2,1)} %vx_in.1, bf16[4,256]{1,0:T(4,128)(2,1)} %vc_in.1, bf16[256,1792]{1,0:T(8,128)(2,1)} %wg_in.1, ...), custom_call_target="tpu_custom_call" | custom-call | tf_op jit(solution)/shard_map/reduce_and_gather/pallas_call | solution.py:389
  63.5 2.2 %gradients.1 = (bf16[256,1792]{1,0:T(8,128)(2,1)}, bf16[256,1792]{1,0:T(8,128)(2,1)}, bf16[1792,256]{1,0:T(8,128)(2,1)}, f32[1,8]{1,0:T(1,128)}) custom-call(bf16[16,6,112,128]{3,2,1,0:T(8,128)(2,1)S(1)} %get-tuple-element.11.full, bf16[2,256,256]{2,1,0:T(8,128)(2,1)S(1)} %get-tuple-element.12.xs, f32[1,8]{1,0:T(1,128)S(1)} %get-tuple-element.13.wts), custom_call_target="tpu_custom_call" | custom-call | tf_op jit(solution)/shard_map/gradients/pallas_call | solution.py:445

commit v6 on v5

--- a/solution.py
+++ b/solution.py
@@ -240,10 +240,11 @@
         arrived(way, s, slab)
         send(ring_d.at[way, s - 1, slab], swap_d.at[dst, slab], ss, rs + slab, across)
 
-    for i in range(4):
-        if i < 3:
-            pass_on(RIGHT, 3, B[i], 0, S_SHORT, R_SHORT)
+    for i in range(3):
         pass_on(LEFT, 3, A[i], 0, S_SHORT, R_SHORT)
+    for i in range(3):
+        pass_on(RIGHT, 3, B[i], 0, S_SHORT, R_SHORT)
+    pass_on(LEFT, 3, 3, 0, S_SHORT, R_SHORT)
     r_row = jnp.zeros((1, TOK), F32)
     for e in range(EX):
         r_row = r_row + jnp.where(ids[...] == e, sw[e], 0.0)
@@ -252,10 +253,11 @@
     got(gram_all.at[c, 0:7], R_GA)
     send(gram_all.at[c], gram_all.at[c], S_GC, R_GC, other)
     got(swap_p, R_P)
-    for i in range(4):
+    for i in range(3):
         pass_on(RIGHT, 4, A[i], 1, S_LONG, R_LONG)
-        if i < 3:
-            pass_on(LEFT, 4, B[i], 1, S_LONG, R_LONG)
+    for i in range(3):
+        pass_on(LEFT, 4, B[i], 1, S_LONG, R_LONG)
+    pass_on(RIGHT, 4, 3, 1, S_LONG, R_LONG)
 
     def whole(slab):
         way = RIGHT if slab < 4 else LEFT
@@ -369,16 +371,31 @@
         copy.wait()
 
 
-def grad_kernel(full, xs, wts, gg, gu, gd, out):
-    def rows(i):
-        return jnp.concatenate(
-            [full[:, i].reshape(8 * HB, 128), full[:, 3 + i].reshape(8 * HB, 128)], axis=1
-        )
+def grad_kernel(full, xs, wts, gg, gu, gd, out, bg, bu, bd, sems):
+    copies = []
+
+    def write(src, dst):
+        copies.append(pltpu.make_async_copy(src, dst, sems.at[len(copies)]))
+        copies[-1].start()
 
     out[...] = wts[...]
-    gd[...] = nt(rows(0), xs[1]).astype(BF)
-    gg[...] = nt(xs[0], rows(1)).astype(BF)
-    gu[...] = nt(xs[0], rows(2)).astype(BF)
+    for h in range(2):
+        part = slice(8 * HB * h, 8 * HB * (h + 1))
+
+        def rows(i):
+            block = full[8 * h : 8 * h + 8]
+            return jnp.concatenate(
+                [block[:, i].reshape(8 * HB, 128), block[:, 3 + i].reshape(8 * HB, 128)], axis=1
+            )
+
+        bd[part] = nt(rows(0), xs[1]).astype(BF)
+        write(bd.at[part], gd.at[part])
+        bg[:, part] = nt(xs[0], rows(1)).astype(BF)
+        write(bg.at[:, part], gg.at[:, part])
+        bu[:, part] = nt(xs[0], rows(2)).astype(BF)
+        write(bu.at[:, part], gu.at[:, part])
+    for copy in copies:
+        copy.wait()
 
 
 def body(train_x, train_cot, val_x, val_cot, w_gate, w_up, w_down, step_weights, example_ids, val_mask):
@@ -444,24 +461,15 @@
     )
     gg, gu, gd, out = pl.pallas_call(
         grad_kernel,
-        grid=(2,),
         out_shape=(
             jax.ShapeDtypeStruct((W, 1792), BF),
             jax.ShapeDtypeStruct((W, 1792), BF),
             jax.ShapeDtypeStruct((1792, W), BF),
             jax.ShapeDtypeStruct((1, EX), F32),
         ),
-        in_specs=[
-            pl.BlockSpec((8, 6, HB, 128), lambda i: (i, 0, 0, 0)),
-            pl.BlockSpec((2, W, TOK), lambda i: (0, 0, 0)),
-            pl.BlockSpec((1, EX), lambda i: (0, 0)),
-        ],
-        out_specs=(
-            pl.BlockSpec((W, 8 * HB), lambda i: (0, i)),
-            pl.BlockSpec((W, 8 * HB), lambda i: (0, i)),
-            pl.BlockSpec((8 * HB, W), lambda i: (i, 0)),
-            pl.BlockSpec((1, EX), lambda i: (0, 0)),
-        ),
+        in_specs=[vmem] * 3,
+        out_specs=(free, free, free, vmem),
+        scratch_shapes=[V((W, 1792), BF), V((W, 1792), BF), V((1792, W), BF), pltpu.SemaphoreType.DMA((6,))],
         compiler_params=pltpu.CompilerParams(vmem_limit_bytes=40 * 1024 * 1024),
         name="gradients",
     )(full, xs, wts)

time: 65.8 us -> 66.1 us (level)
  no operation moved by 1% of the time
where the time goes in v6:
time: 66.1 us; the launch traced here: 66 us
  Pallas kernels  65.4 us (99%)
    pallas_call x1, Pallas kernels, body(): pl.pallas_call(comm_kernel, out_shape=(jax.ShapeDtypeStruct((16, 6, HB, 1...  62.9 us
    pallas_call x1, Pallas kernels, body(): pl.pallas_call(grad_kernel, out_shape=(jax.ShapeDtypeStruct((W, 1792), BF...  2.52 us

profile of v6, /device:TPU:1, one launch (start us, length us, event | category | flops | bytes accessed | tf_op | source)
XLA Modules:
  0.0 66.0 jit_solution(17139909038655813406)
XLA Ops:
  0.6 62.9 %reduce_and_gather.1 = (bf16[16,6,112,128]{3,2,1,0:T(8,128)(2,1)S(1)}, bf16[2,256,256]{2,1,0:T(8,128)(2,1)S(1)}, f32[1,8]{1,0:T(1,128)S(1)}) custom-call(bf16[32,256]{1,0:T(8,128)(2,1)} %x_in.1, bf16[32,256]{1,0:T(8,128)(2,1)} %c_in.1, bf16[4,256]{1,0:T(4,128)(2,1)} %vx_in.1, bf16[4,256]{1,0:T(4,128)(2,1)} %vc_in.1, bf16[256,1792]{1,0:T(8,128)(2,1)} %wg_in.1, ...), custom_call_target="tpu_custom_call" | custom-call | tf_op jit(solution)/shard_map/reduce_and_gather/pallas_call | solution.py:406
  63.5 2.5 %gradients.1 = (bf16[256,1792]{1,0:T(8,128)(2,1)}, bf16[256,1792]{1,0:T(8,128)(2,1)}, bf16[1792,256]{1,0:T(8,128)(2,1)}, f32[1,8]{1,0:T(1,128)}) custom-call(bf16[16,6,112,128]{3,2,1,0:T(8,128)(2,1)S(1)} %get-tuple-element.11.full, bf16[2,256,256]{2,1,0:T(8,128)(2,1)S(1)} %get-tuple-element.12.xs, f32[1,8]{1,0:T(1,128)S(1)} %get-tuple-element.13.wts), custom_call_target="tpu_custom_call" | custom-call | tf_op jit(solution)/shard_map/gradients/pallas_call | solution.py:462

commit v7 on v5

--- a/solution.py
+++ b/solution.py
@@ -66,13 +66,18 @@
         pltpu.make_async_copy(dst, dst, rsem.at[rs]).wait()
 
     R_X, R_XO, R_W, R_P, R_GS, R_GX, R_GA, R_GC, R_AC, R_S1, R_S2, R_S3 = 0, 8, 9, 11, 12, 13, 14, 15, 16, 17, 18, 19
-    R_SHORT, R_LONG, R_RING, R_A = 20, 27, 34, 83
-
-    (S_X, S_W, S_XO, S_RING, S_LAST, S_P, S_SHORT, S_LONG, S_GS, S_GX, S_GA, S_GC, S_A, S_AC, S_S1, S_S2, S_S3) = range(17)
+    R_SHORT, R_LONG, R_RING, R_A, R_Y, R_YO = 20, 27, 34, 83, 125, 133
+
+    (S_X, S_W, S_XO, S_RING, S_LAST, S_P, S_SHORT, S_LONG, S_GS, S_GX, S_GA, S_GC, S_A, S_AC, S_S1, S_S2, S_S3, S_Y, S_YO) = range(19)
+
+    barrier = pltpu.get_barrier_semaphore()
+    peers = [mdev(k) for k in range(1, NM)] + [across, other] + [zdev(k) for k in range(1, NZ)]
+    for peer in peers:
+        pl.semaphore_signal(barrier, inc=1, device_id=peer, device_id_type=MESH)
 
     loads = [
         pltpu.make_async_copy(x_in, pk.at[0:32], lsem.at[0]),
-        pltpu.make_async_copy(c_in, pk.at[32:64], lsem.at[1]),
+        pltpu.make_async_copy(c_in, pk.at[48:80], lsem.at[1]),
         pltpu.make_async_copy(wg_in, wraw.at[0], lsem.at[2]),
         pltpu.make_async_copy(wu_in, wraw.at[1], lsem.at[3]),
         pltpu.make_async_copy(vx_in, vraw.at[0], lsem.at[4]),
@@ -86,26 +91,24 @@
     for copy in loads:
         copy.start()
 
-    barrier = pltpu.get_barrier_semaphore()
-    peers = [mdev(k) for k in range(1, NM)] + [across, other] + [zdev(k) for k in range(1, NZ)]
-    for peer in peers:
-        pl.semaphore_signal(barrier, inc=1, device_id=peer, device_id_type=MESH)
-
     vstage[0:16] = jnp.zeros((16, W), F32)
     loads[4].wait()
     loads[5].wait()
     vstage[0:4] = vraw[0].astype(F32)
     vstage[4:8] = vraw[0].astype(F32)
     vstage[8:12] = vraw[1].astype(F32)
-    pk[64:80] = vstage[0:16].astype(BF)
+    pk[32:48] = vstage[0:16].astype(BF)
     loads[0].wait()
     loads[1].wait()
     xb[m] = pk[...]
     pl.semaphore_wait(barrier, len(peers))
 
-    for k in range(1, NM):
-        send(pk, xb.at[m], S_X, R_X + m, mdev(k))
-    send(pk, xo.at[m], S_X, R_XO, other)
+    for k in (4, 3, 5, 2, 6, 1, 7):
+        send(pk.at[0:48], xb.at[m, 0:48], S_X, R_X + m, mdev(k))
+    send(pk.at[0:48], xo.at[m, 0:48], S_X, R_XO, other)
+    for k in (4, 3, 5, 2, 6, 1, 7):
+        send(pk.at[48:80], xb.at[m, 48:80], S_Y, R_Y + m, mdev(k))
+    send(pk.at[48:80], xo.at[m, 48:80], S_Y, R_YO, other)
 
     for w in range(2):
         loads[2 + w].wait()
@@ -122,31 +125,34 @@
     for step in (4, 3, 5, 2, 6, 1, 7, 0):
         send(wt.at[1 - c, at(step)], wo.at[at(step)], S_W, R_W if step == 4 else R_W + 1, other)
 
-    for k in range(1, NM):
+    for k in (1, 7, 2, 6, 3, 5, 4):
         j = (m + NM - k) % NM
-        got(xb.at[j], R_X + j)
-        send(xb.at[j], xo.at[j], S_XO, R_XO, other)
+        got(xb.at[j, 0:48], R_X + j)
+        send(xb.at[j, 0:48], xo.at[j, 0:48], S_XO, R_XO, other)
     place = lax.broadcasted_iota(jnp.int32, (128, W), 0) % 16
 
     def spread(src, dst):
-        rows = src[:, 64:80, :].reshape(128, W).astype(F32)
+        rows = src[:, 32:48, :].reshape(128, W).astype(F32)
         for i in range(3):
             keep = jnp.logical_and(place >= 4 * i, place < 4 * i + 4)
             dst[i] = jnp.where(keep, rows, 0.0).astype(BF)
 
     def tokens(ref, first):
-        return ref[:, 32 * first : 32 * first + 32, :].reshape(TOK, W)
-
-    spread(xb, va)
-    val = jnp.zeros((NZ * HB, 128), F32)
-    for i in range(3):
+        return ref[:, 48 * first : 48 * first + 32, :].reshape(TOK, W)
+
+    def own_width(i):
         lhs = wt[c, :, i].reshape(NZ * HB, W)
         total = nt(lhs, tokens(xb, 1 if i == 2 else 0))
         part[:, i] = total[:, :128].reshape(NZ, HB, 128)
         part[:, 4 + i] = total[:, 128:].reshape(NZ, HB, 128)
-        val = val + nt(lhs, va[i])
-    part[:, 3] = val.reshape(NZ, HB, 128)
-    got(xo, R_XO)
+
+    own_width(0)
+    own_width(1)
+    for k in (1, 7, 2, 6, 3, 5, 4):
+        j = (m + NM - k) % NM
+        got(xb.at[j, 48:80], R_Y + j)
+        send(xb.at[j, 48:80], xo.at[j, 48:80], S_YO, R_YO, other)
+    got(xo.at[:, 0:48], R_XO)
 
     A, B = (0, 1, 2, 3), (4, 5, 6)
     RIGHT, LEFT = 0, 1
@@ -177,13 +183,17 @@
     far = at(4)
     got(wo.at[far], R_W)
     for i in range(3):
+        if i == 2:
+            own_width(2)
+            got(xo.at[:, 48:80], R_YO)
         total = nt(wo[far, i], tokens(xo, 1 if i == 2 else 0))
         first(RIGHT, i, part[far, i] + total[:, :128])
         first(LEFT, 4 + i, part[far, 4 + i] + total[:, 128:])
+    spread(xb, va)
     spread(xo, vo)
-    val = part[far, 3]
-    for i in range(3):
-        val = val + nt(wo[far, i], vo[i])
+    val = jnp.zeros((HB, 128), F32)
+    for i in range(3):
+        val = val + nt(wt[c, far, i], va[i]) + nt(wo[far, i], vo[i])
     first(RIGHT, 3, val)
 
     got(wo.at[0:7], R_W + 1)
@@ -195,8 +205,8 @@
         part[:, 4 + i] = part[:, 4 + i] + total[:, 128:].reshape(NZ, HB, 128)
         first(LEFT, i, part[at(-3), i])
         first(RIGHT, 4 + i, part[at(3), 4 + i])
-        val = val + nt(lhs, vo[i])
-    part[:, 3] = part[:, 3] + val.reshape(NZ, HB, 128)
+        val = val + nt(lhs, vo[i]) + nt(wt[c, :, i].reshape(NZ * HB, W), va[i])
+    part[:, 3] = val.reshape(NZ, HB, 128)
     first(LEFT, 3, part[at(-3), 3])
     send(part.at[z], swap_p, S_P, R_P, across)
 
@@ -213,7 +223,7 @@
             onward(LEFT, s, A[i], s - 3)
 
     def half(ref, which):
-        return ref[pl.ds(4 * c, 4), 32 * which : 32 * which + 32, :].reshape(128, W)
+        return ref[pl.ds(4 * c, 4), 48 * which : 48 * which + 32, :].reshape(128, W)
 
     gram = nt(va[0], half(xb, 0)) + nt(vo[0], half(xo, 0)) + nt(va[2], half(xb, 1)) + nt(vo[2], half(xo, 1))
     gram_s[...] = gram.reshape(NZ, 16, 128)
@@ -240,10 +250,11 @@
         arrived(way, s, slab)
         send(ring_d.at[way, s - 1, slab], swap_d.at[dst, slab], ss, rs + slab, across)
 
-    for i in range(4):
-        if i < 3:
-            pass_on(RIGHT, 3, B[i], 0, S_SHORT, R_SHORT)
+    for i in range(3):
         pass_on(LEFT, 3, A[i], 0, S_SHORT, R_SHORT)
+    for i in range(3):
+        pass_on(RIGHT, 3, B[i], 0, S_SHORT, R_SHORT)
+    pass_on(LEFT, 3, 3, 0, S_SHORT, R_SHORT)
     r_row = jnp.zeros((1, TOK), F32)
     for e in range(EX):
         r_row = r_row + jnp.where(ids[...] == e, sw[e], 0.0)
@@ -252,10 +263,11 @@
     got(gram_all.at[c, 0:7], R_GA)
     send(gram_all.at[c], gram_all.at[c], S_GC, R_GC, other)
     got(swap_p, R_P)
-    for i in range(4):
+    for i in range(3):
         pass_on(RIGHT, 4, A[i], 1, S_LONG, R_LONG)
-        if i < 3:
-            pass_on(LEFT, 4, B[i], 1, S_LONG, R_LONG)
+    for i in range(3):
+        pass_on(LEFT, 4, B[i], 1, S_LONG, R_LONG)
+    pass_on(RIGHT, 4, 3, 1, S_LONG, R_LONG)
 
     def whole(slab):
         way = RIGHT if slab < 4 else LEFT
@@ -290,18 +302,19 @@
 
     def step_of_gather(step):
         blocks = [2 * at(-step) + c, 2 * at(step) + c]
-        for i in range(6):
+        order = (0, 3, 1, 4, 2, 5) if step == 4 else range(6)
+        for i in order:
             for way in (RIGHT, LEFT):
                 if step == 4 and i // 3 != way:
                     continue
                 got(full.at[blocks[way], i], gather_sem(way, step, i))
                 if step < 3 or (step == 3 and i // 3 == way):
                     gather(full.at[blocks[way], i], blocks[way], way, step + 1, i)
+                if step == 4:
+                    send(full.at[blocks[way], i], full.at[blocks[way], i], S_AC, R_AC, other)
         if step < 4:
             for way in (RIGHT, LEFT):
                 send(full.at[blocks[way]], full.at[blocks[way]], S_AC, R_AC, other)
-        else:
-            send(full.at[blocks[0]], full.at[blocks[0]], S_AC, R_AC, other)
 
     got(gram_all.at[1 - c], R_GC)
     kt = jnp.concatenate([gram_all[0].reshape(128, 128), gram_all[1].reshape(128, 128)], axis=1)
@@ -359,7 +372,7 @@
     step_of_gather(4)
     got(full.at[0:8], R_AC)
     for ref, ss in (
-        (xb, S_X), (wo, S_W), (xb.at[0:7], S_XO), (ring_s.at[:, 0:3], S_RING), (swap_d.at[0], S_LAST), (swap_p, S_P),
+        (xb.at[:, 0:48], S_X), (xb.at[:, 48:80], S_Y), (wo, S_W), (xb.at[0:7, 0:48], S_XO), (xb.at[0:7, 48:80], S_YO), (ring_s.at[:, 0:3], S_RING), (swap_d.at[0], S_LAST), (swap_p, S_P),
         (swap_d.at[0], S_SHORT), (swap_d.at[1], S_LONG), (gram_d.at[0:7], S_GS), (gram_x.at[0], S_GX),
         (gram_all.at[0, 0:7], S_GA), (gram_all.at[0], S_GC), (full.at[0:7], S_A), (full.at[0:8], S_AC),
         (sc1.at[0:7], S_S1), (sc2.at[0], S_S2), (sc3.at[0:7], S_S3),
@@ -369,7 +382,9 @@
         copy.wait()
 
 
-def grad_kernel(full, xs, wts, gg, gu, gd, out):
+def grad_kernel(whole, xs, wts, gg, gu, gd, out):
+    full = whole[pl.ds(8 * pl.program_id(0), 8)]
+
     def rows(i):
         return jnp.concatenate(
             [full[:, i].reshape(8 * HB, 128), full[:, 3 + i].reshape(8 * HB, 128)], axis=1
@@ -425,8 +440,8 @@
             V((2, W, TOK), F32),
             V((2, W, TOK), BF),
             pltpu.SemaphoreType.DMA((11,)),
-            pltpu.SemaphoreType.DMA((17,)),
-            pltpu.SemaphoreType.DMA((125,)),
+            pltpu.SemaphoreType.DMA((19,)),
+            pltpu.SemaphoreType.DMA((134,)),
             pltpu.SemaphoreType.DMA((2,)),
         ],
         compiler_params=pltpu.CompilerParams(
@@ -452,9 +467,9 @@
             jax.ShapeDtypeStruct((1, EX), F32),
         ),
         in_specs=[
-            pl.BlockSpec((8, 6, HB, 128), lambda i: (i, 0, 0, 0)),
-            pl.BlockSpec((2, W, TOK), lambda i: (0, 0, 0)),
-            pl.BlockSpec((1, EX), lambda i: (0, 0)),
+            vmem,
+            vmem,
+            vmem,
         ],
         out_specs=(
             pl.BlockSpec((W, 8 * HB), lambda i: (0, i)),

time: 65.8 us -> 64.8 us (0.985)
  Pallas kernels: 65.1 us -> 64.1 us
    pallas_call x1, Pallas kernels: 62.9 us -> 61.9 us  [body(): pl.pallas_call(comm_kernel, out_shape=(jax.ShapeDtypeStruct((16, 6, HB, 1...]
where the time goes in v7:
time: 64.8 us; the launch traced here: 64.7 us
  Pallas kernels  64.1 us (99%)
    pallas_call x1, Pallas kernels, body(): pl.pallas_call(comm_kernel, out_shape=(jax.ShapeDtypeStruct((16, 6, HB, 1...  61.9 us
    pallas_call x1, Pallas kernels, body(): pl.pallas_call(grad_kernel, grid=(2,), out_shape=(jax.ShapeDtypeStruct((W...  2.19 us

profile of v7, /device:TPU:1, one launch (start us, length us, event | category | flops | bytes accessed | tf_op | source)
XLA Modules:
  0.0 64.7 jit_solution(11313668311993108889)
XLA Ops:
  0.6 61.9 %reduce_and_gather.1 = (bf16[16,6,112,128]{3,2,1,0:T(8,128)(2,1)S(1)}, bf16[2,256,256]{2,1,0:T(8,128)(2,1)S(1)}, f32[1,8]{1,0:T(1,128)S(1)}) custom-call(bf16[32,256]{1,0:T(8,128)(2,1)} %x_in.1, bf16[32,256]{1,0:T(8,128)(2,1)} %c_in.1, bf16[4,256]{1,0:T(4,128)(2,1)} %vx_in.1, bf16[4,256]{1,0:T(4,128)(2,1)} %vc_in.1, bf16[256,1792]{1,0:T(8,128)(2,1)} %wg_in.1, ...), custom_call_target="tpu_custom_call" | custom-call | tf_op jit(solution)/shard_map/reduce_and_gather/pallas_call | solution.py:404
  62.5 2.2 %gradients.1 = (bf16[256,1792]{1,0:T(8,128)(2,1)}, bf16[256,1792]{1,0:T(8,128)(2,1)}, bf16[1792,256]{1,0:T(8,128)(2,1)}, f32[1,8]{1,0:T(1,128)}) custom-call(bf16[16,6,112,128]{3,2,1,0:T(8,128)(2,1)S(1)} %get-tuple-element.11.whole, bf16[2,256,256]{2,1,0:T(8,128)(2,1)S(1)} %get-tuple-element.12.xs, f32[1,8]{1,0:T(1,128)S(1)} %get-tuple-element.13.wts), custom_call_target="tpu_custom_call" | custom-call | tf_op jit(solution)/shard_map/gradients/pallas_call | solution.py:460

commit v8 on v7

--- a/solution.py
+++ b/solution.py
@@ -66,7 +66,7 @@
         pltpu.make_async_copy(dst, dst, rsem.at[rs]).wait()
 
     R_X, R_XO, R_W, R_P, R_GS, R_GX, R_GA, R_GC, R_AC, R_S1, R_S2, R_S3 = 0, 8, 9, 11, 12, 13, 14, 15, 16, 17, 18, 19
-    R_SHORT, R_LONG, R_RING, R_A, R_Y, R_YO = 20, 27, 34, 83, 125, 133
+    R_SHORT, R_LONG, R_RING, R_A, R_Y, R_YO = 20, 23, 26, 75, 117, 118
 
     (S_X, S_W, S_XO, S_RING, S_LAST, S_P, S_SHORT, S_LONG, S_GS, S_GX, S_GA, S_GC, S_A, S_AC, S_S1, S_S2, S_S3, S_Y, S_YO) = range(19)
 
@@ -107,7 +107,7 @@
         send(pk.at[0:48], xb.at[m, 0:48], S_X, R_X + m, mdev(k))
     send(pk.at[0:48], xo.at[m, 0:48], S_X, R_XO, other)
     for k in (4, 3, 5, 2, 6, 1, 7):
-        send(pk.at[48:80], xb.at[m, 48:80], S_Y, R_Y + m, mdev(k))
+        send(pk.at[48:80], xb.at[m, 48:80], S_Y, R_Y, mdev(k))
     send(pk.at[48:80], xo.at[m, 48:80], S_Y, R_YO, other)
 
     for w in range(2):
@@ -148,9 +148,9 @@
 
     own_width(0)
     own_width(1)
+    got(xb.at[0:7, 48:80], R_Y)
     for k in (1, 7, 2, 6, 3, 5, 4):
         j = (m + NM - k) % NM
-        got(xb.at[j, 48:80], R_Y + j)
         send(xb.at[j, 48:80], xo.at[j, 48:80], S_YO, R_YO, other)
     got(xo.at[:, 0:48], R_XO)
 
@@ -211,16 +211,16 @@
     send(part.at[z], swap_p, S_P, R_P, across)
 
     def both_long(s):
-        for i in range(4):
+        for i in range(3):
             onward(RIGHT, s, A[i], 4 - s)
-            if i < 3:
-                onward(LEFT, s, B[i], s - 4)
+            onward(LEFT, s, B[i], s - 4)
 
     def both_short(s):
-        for i in range(4):
-            if i < 3:
-                onward(RIGHT, s, B[i], 3 - s)
+        for i in range(3):
+            onward(RIGHT, s, B[i], 3 - s)
             onward(LEFT, s, A[i], s - 3)
+        onward(RIGHT, s, 3, 4 - s)
+        onward(LEFT, s, 3, s - 3)
 
     def half(ref, which):
         return ref[pl.ds(4 * c, 4), 48 * which : 48 * which + 32, :].reshape(128, W)
@@ -235,45 +235,48 @@
     both_short(1)
     for copy in loads[8:]:
         copy.wait()
+    both_long(2)
+    both_short(2)
     got(gram_d.at[0:7], R_GS)
     gram_x[0] = jnp.sum(gram_d[...], axis=0)
     send(gram_x.at[0], gram_x.at[1], S_GX, R_GX, across)
-    both_long(2)
-    both_short(2)
-    got(gram_x.at[1], R_GX)
-    gram_all[c, z] = gram_x[0] + gram_x[1]
-    for k in range(1, NZ):
-        send(gram_all.at[c, z], gram_all.at[c, z], S_GA, R_GA, zdev(k))
     both_long(3)
 
     def pass_on(way, s, slab, dst, ss, rs):
         arrived(way, s, slab)
-        send(ring_d.at[way, s - 1, slab], swap_d.at[dst, slab], ss, rs + slab, across)
+        send(ring_d.at[way, s - 1, slab], swap_d.at[dst, slab], ss, rs + (0, 0, 0, 1, 2, 2, 2)[slab], across)
 
     for i in range(3):
         pass_on(LEFT, 3, A[i], 0, S_SHORT, R_SHORT)
     for i in range(3):
         pass_on(RIGHT, 3, B[i], 0, S_SHORT, R_SHORT)
+    onward(RIGHT, 3, 3, 1)
     pass_on(LEFT, 3, 3, 0, S_SHORT, R_SHORT)
     r_row = jnp.zeros((1, TOK), F32)
     for e in range(EX):
         r_row = r_row + jnp.where(ids[...] == e, sw[e], 0.0)
     for i in range(2):
         xt[i] = tokens(xb, i).T.astype(F32)
+    got(gram_x.at[1], R_GX)
+    gram_all[c, z] = gram_x[0] + gram_x[1]
+    for k in range(1, NZ):
+        send(gram_all.at[c, z], gram_all.at[c, z], S_GA, R_GA, zdev(k))
+    got(swap_p, R_P)
+    for i in range(3):
+        pass_on(RIGHT, 4, A[i], 1, S_LONG, R_LONG)
+    for i in range(3):
+        pass_on(LEFT, 4, B[i], 1, S_LONG, R_LONG)
+    pass_on(RIGHT, 4, 3, 1, S_LONG, R_LONG)
     got(gram_all.at[c, 0:7], R_GA)
     send(gram_all.at[c], gram_all.at[c], S_GC, R_GC, other)
-    got(swap_p, R_P)
-    for i in range(3):
-        pass_on(RIGHT, 4, A[i], 1, S_LONG, R_LONG)
-    for i in range(3):
-        pass_on(LEFT, 4, B[i], 1, S_LONG, R_LONG)
-    pass_on(RIGHT, 4, 3, 1, S_LONG, R_LONG)
+
+    def passed(group, slab, count):
+        got(swap_d.at[0, slab : slab + count], R_SHORT + group)
+        got(swap_d.at[1, slab : slab + count], R_LONG + group)
 
     def whole(slab):
         way = RIGHT if slab < 4 else LEFT
         mine_ = part[z, slab] + ring_d[1 - way, 2, slab].astype(F32) + ring_d[way, 3, slab].astype(F32)
-        got(swap_d.at[0, slab], R_SHORT + slab)
-        got(swap_d.at[1, slab], R_LONG + slab)
         theirs = swap_p[slab] + swap_d[0, slab].astype(F32) + swap_d[1, slab].astype(F32)
         return mine_ + theirs
 
@@ -291,6 +294,7 @@
         send(src, full.at[block, slab], S_A, gather_sem(way, step, slab), to_dev[way])
 
     for h in range(2):
+        passed(2 * h, 4 * h, 3)
         terms = block_terms(*[whole(4 * h + i) for i in range(3)])
         for i in range(3):
             own[3 * h + i] = terms[i].astype(BF)
@@ -320,6 +324,7 @@
     kt = jnp.concatenate([gram_all[0].reshape(128, 128), gram_all[1].reshape(128, 128)], axis=1)
     rk = (kt * r_row).astype(BF)
     hb, dgb, dub = [jnp.concatenate([own[i], own[3 + i]], axis=1) for i in range(3)]
+    passed(1, 3, 1)
     val = whole(3)
     v_gate = val - LEARN_RATE * nt(dgb, rk)
     v_up = pltpu.roll(val, 124, 1) - LEARN_RATE * nt(dub, rk)
@@ -441,7 +446,7 @@
             V((2, W, TOK), BF),
             pltpu.SemaphoreType.DMA((11,)),
             pltpu.SemaphoreType.DMA((19,)),
-            pltpu.SemaphoreType.DMA((134,)),
+            pltpu.SemaphoreType.DMA((119,)),
             pltpu.SemaphoreType.DMA((2,)),
         ],
         compiler_params=pltpu.CompilerParams(

time: 64.8 us -> 64.7 us (level)
  no operation moved by 1% of the time
where the time goes in v8:
time: 64.7 us; the launch traced here: 64.6 us
  Pallas kernels  64 us (99%)
    pallas_call x1, Pallas kernels, body(): pl.pallas_call(comm_kernel, out_shape=(jax.ShapeDtypeStruct((16, 6, HB, 1...  61.8 us
    pallas_call x1, Pallas kernels, body(): pl.pallas_call(grad_kernel, grid=(2,), out_shape=(jax.ShapeDtypeStruct((W...  2.19 us

profile of v8, /device:TPU:1, one launch (start us, length us, event | category | flops | bytes accessed | tf_op | source)
XLA Modules:
  0.0 64.6 jit_solution(17764545482741967348)
XLA Ops:
  0.6 61.8 %reduce_and_gather.1 = (bf16[16,6,112,128]{3,2,1,0:T(8,128)(2,1)S(1)}, bf16[2,256,256]{2,1,0:T(8,128)(2,1)S(1)}, f32[1,8]{1,0:T(1,128)S(1)}) custom-call(bf16[32,256]{1,0:T(8,128)(2,1)} %x_in.1, bf16[32,256]{1,0:T(8,128)(2,1)} %c_in.1, bf16[4,256]{1,0:T(4,128)(2,1)} %vx_in.1, bf16[4,256]{1,0:T(4,128)(2,1)} %vc_in.1, bf16[256,1792]{1,0:T(8,128)(2,1)} %wg_in.1, ...), custom_call_target="tpu_custom_call" | custom-call | tf_op jit(solution)/shard_map/reduce_and_gather/pallas_call | solution.py:409
  62.4 2.2 %gradients.1 = (bf16[256,1792]{1,0:T(8,128)(2,1)}, bf16[256,1792]{1,0:T(8,128)(2,1)}, bf16[1792,256]{1,0:T(8,128)(2,1)}, f32[1,8]{1,0:T(1,128)}) custom-call(bf16[16,6,112,128]{3,2,1,0:T(8,128)(2,1)S(1)} %get-tuple-element.11.whole, bf16[2,256,256]{2,1,0:T(8,128)(2,1)S(1)} %get-tuple-element.12.xs, f32[1,8]{1,0:T(1,128)S(1)} %get-tuple-element.13.wts), custom_call_target="tpu_custom_call" | custom-call | tf_op jit(solution)/shard_map/gradients/pallas_call | solution.py:465

commit v9 on v8

--- a/solution.py
+++ b/solution.py
@@ -66,7 +66,7 @@
         pltpu.make_async_copy(dst, dst, rsem.at[rs]).wait()
 
     R_X, R_XO, R_W, R_P, R_GS, R_GX, R_GA, R_GC, R_AC, R_S1, R_S2, R_S3 = 0, 8, 9, 11, 12, 13, 14, 15, 16, 17, 18, 19
-    R_SHORT, R_LONG, R_RING, R_A, R_Y, R_YO = 20, 23, 26, 75, 117, 118
+    R_SHORT, R_LONG, R_RING, R_A, R_Y, R_YO = 20, 23, 26, 75, 93, 94
 
     (S_X, S_W, S_XO, S_RING, S_LAST, S_P, S_SHORT, S_LONG, S_GS, S_GX, S_GA, S_GC, S_A, S_AC, S_S1, S_S2, S_S3, S_Y, S_YO) = range(19)
 
@@ -286,9 +286,9 @@
         return act * up, back * up * sig * (1.0 + gate * (1.0 - sig)), back * act
 
     def gather_sem(way, step, slab):
-        if step < 4:
-            return R_A + (way * 3 + step - 1) * 6 + slab
-        return R_A + 36 + slab
+        if step < 3:
+            return ring_sem(way, step - 1, slab)
+        return R_A + (way * 6 + slab if step == 3 else 12 + slab)
 
     def gather(src, block, way, step, slab):
         send(src, full.at[block, slab], S_A, gather_sem(way, step, slab), to_dev[way])
@@ -446,7 +446,7 @@
             V((2, W, TOK), BF),
             pltpu.SemaphoreType.DMA((11,)),
             pltpu.SemaphoreType.DMA((19,)),
-            pltpu.SemaphoreType.DMA((119,)),
+            pltpu.SemaphoreType.DMA((95,)),
             pltpu.SemaphoreType.DMA((2,)),
         ],
         compiler_params=pltpu.CompilerParams(

time: 64.7 us -> 64.5 us (level)
  no operation moved by 1% of the time
where the time goes in v9:
time: 64.5 us; the launch traced here: 64.4 us
  Pallas kernels  63.8 us (99%)
    pallas_call x1, Pallas kernels, body(): pl.pallas_call(comm_kernel, out_shape=(jax.ShapeDtypeStruct((16, 6, HB, 1...  61.6 us
    pallas_call x1, Pallas kernels, body(): pl.pallas_call(grad_kernel, grid=(2,), out_shape=(jax.ShapeDtypeStruct((W...  2.18 us

profile of v9, /device:TPU:1, one launch (start us, length us, event | category | flops | bytes accessed | tf_op | source)
XLA Modules:
  0.0 64.4 jit_solution(2100775162172928295)
XLA Ops:
  0.6 61.6 %reduce_and_gather.1 = (bf16[16,6,112,128]{3,2,1,0:T(8,128)(2,1)S(1)}, bf16[2,256,256]{2,1,0:T(8,128)(2,1)S(1)}, f32[1,8]{1,0:T(1,128)S(1)}) custom-call(bf16[32,256]{1,0:T(8,128)(2,1)} %x_in.1, bf16[32,256]{1,0:T(8,128)(2,1)} %c_in.1, bf16[4,256]{1,0:T(4,128)(2,1)} %vx_in.1, bf16[4,256]{1,0:T(4,128)(2,1)} %vc_in.1, bf16[256,1792]{1,0:T(8,128)(2,1)} %wg_in.1, ...), custom_call_target="tpu_custom_call" | custom-call | tf_op jit(solution)/shard_map/reduce_and_gather/pallas_call | solution.py:409
  62.2 2.2 %gradients.1 = (bf16[256,1792]{1,0:T(8,128)(2,1)}, bf16[256,1792]{1,0:T(8,128)(2,1)}, bf16[1792,256]{1,0:T(8,128)(2,1)}, f32[1,8]{1,0:T(1,128)}) custom-call(bf16[16,6,112,128]{3,2,1,0:T(8,128)(2,1)S(1)} %get-tuple-element.11.whole, bf16[2,256,256]{2,1,0:T(8,128)(2,1)S(1)} %get-tuple-element.12.xs, f32[1,8]{1,0:T(1,128)S(1)} %get-tuple-element.13.wts), custom_call_target="tpu_custom_call" | custom-call | tf_op jit(solution)/shard_map/gradients/pallas_call | solution.py:465
